TPU v7x, 128 devices: a whole 4x4x4 slice. The times are simulated.
128 devices in a mesh: lat: 8 (over z, x_lo), lon: 16 (over x_hi, y, core).
Axes of the slice: x: 4 (x_hi: 2, x_lo: 2; x = x_hi * 2 + x_lo), y: 4, z: 4, core: 2. Of those that a mesh axis runs over, the one named last changes fastest.
Arguments:
- tokens: bfloat16 [2, 96, 192, 1024], P(None, 'lat', 'lon'), may hold values from -37 to 37
- masked: int32 [8, 16, 144], P('lat', 'lon'), may hold values from 0 to 287, all different within a row
- mask_embed: bfloat16 [1024], replicated, may hold values from -6 to 6
- w_qkv: bfloat16 [1024, 3072], replicated
- w_out: bfloat16 [1024, 1024], replicated, may hold values from -0.1875 to 0.1875
- cotangent: bfloat16 [2, 96, 192, 1024], P(None, 'lat', 'lon'), may hold values from -6 to 6
Outputs:
- block_out: bfloat16 [2, 96, 192, 1024], P(None, 'lat', 'lon')
- grad_tokens: bfloat16 [2, 96, 192, 1024], P(None, 'lat', 'lon')
- grad_qkv: float32 [1024, 3072], P(('lat', 'lon'))
- grad_out: float32 [1024, 1024], P(('lat', 'lon'))
- grad_mask: float32 [1024], P(('lat', 'lon'))
Inputs may be any that keep to these rules, and one draw needn't show every extreme that they name: `masked`: within each tile the 144 listed positions are all different.
All inputs are finite; a program needn't handle non-finite values.
Results may differ from a plain program's by a relative error of at most 0.012.
The roundings to bfloat16 on the way count: a program that leaves them out, or rounds other values in their place, can miss the bound.
Values may be sent and summed in bfloat16 or wider, within the bound.
A program may use at most 128 MiB of HBM per device.

v0:
```python
import math

import jax
import jax.numpy as jnp
import numpy as np
from jax import lax
from jax.experimental import pallas as pl
from jax.experimental.pallas import tpu as pltpu
from jax.sharding import PartitionSpec as P

HEADS = 16
MESH = pl.DeviceIdType.MESH
BF16 = jnp.bfloat16
F32 = jnp.float32


def piece_order():
    column, row, lev = np.meshgrid(np.arange(12), np.arange(6), np.arange(2), indexing="ij")
    top = (column * 24 + row * 2 + lev).reshape(-1)
    return np.concatenate([top, top + 12])


def middle_order():
    column, row, lev = np.meshgrid(np.arange(12), np.arange(24), np.arange(2), indexing="ij")
    north = column * 12 + row * 2 + lev
    inside = 144 + column * 24 + (row - 6) * 2 + lev
    south = 432 + column * 12 + (row - 18) * 2 + lev
    return np.where(row < 6, north, np.where(row < 18, inside, south)).reshape(-1)


def one_hot(order):
    return (order[:, None] == np.arange(order.size)[None, :]).astype(np.float32)


def near():
    query = np.arange(96)
    key = np.arange(768)
    row, column = query % 24 // 2, query // 24
    krow, kcolumn = key % 48 // 2, key // 48
    allowed = (krow[None] >= row[:, None]) & (krow[None] <= row[:, None] + 11)
    return allowed & (kcolumn[None] >= column[:, None]) & (kcolumn[None] <= column[:, None] + 11)


def dot(a, b):
    return jnp.dot(a, b, preferred_element_type=F32)


def dot_nt(a, b):
    return lax.dot_general(a, b, (((1,), (1,)), ((), ())), preferred_element_type=F32)


def dot_tn(a, b):
    return lax.dot_general(a, b, (((0,), (0,)), ((), ())), preferred_element_type=F32)


def attention_kernel(
    xm, g, w_qkv, w_out, bias, to_piece, from_piece, to_middle, from_middle,
    ctx, dqkv,
    pieces, stacked, ext, q, d, kv, acc, side_out, side_in, piece_out, piece_in, own,
    send, recv,
):
    lat, lon = lax.axis_index("lat"), lax.axis_index("lon")
    north, south = (lax.rem(lat + 7, 8), lon), (lax.rem(lat + 1, 8), lon)
    west, east = (lat, lax.rem(lon + 15, 16)), (lat, lax.rem(lon + 1, 16))
    barrier = pltpu.get_barrier_semaphore()
    for neighbour in (north, south, west, east):
        pl.semaphore_signal(barrier, inc=1, device_id=neighbour, device_id_type=MESH)

    pieces[...] = dot(to_piece[...], xm[...]).astype(BF16)
    stacked[144:432, :] = xm[...]
    pl.semaphore_wait(barrier, 4)

    def copy_to(source, target, sem, device):
        return pltpu.make_async_remote_copy(
            src_ref=source,
            dst_ref=target,
            send_sem=send.at[sem],
            recv_sem=recv.at[sem],
            device_id=device,
            device_id_type=MESH,
        )

    def part(start, rows):
        return pl.ds(start, rows)

    first = (
        copy_to(pieces.at[part(0, 144)], stacked.at[part(432, 144)], 0, north),
        copy_to(pieces.at[part(144, 144)], stacked.at[part(0, 144)], 1, south),
    )
    for copy in first:
        copy.start()

    @pl.loop(0, 4)
    def _(t):
        cols = pl.ds(pl.multiple_of(t * 256, 256), 256)
        q[:, cols] = dot(xm[...], w_qkv[:, cols]).astype(BF16)
        d[:, cols] = dot_nt(g[...], w_out[cols, :]).astype(BF16)

    for copy in first:
        copy.wait()
    ext[288:864, :] = dot(to_middle[...], stacked[...]).astype(BF16)
    second = (
        copy_to(ext.at[part(288, 288)], ext.at[part(864, 288)], 2, west),
        copy_to(ext.at[part(576, 288)], ext.at[part(0, 288)], 3, east),
    )
    for copy in second:
        copy.start()

    def project(start, rows):
        @pl.loop(0, 8)
        def _(t):
            cols = pl.ds(pl.multiple_of(t * 256, 256), 256)
            from_cols = pl.ds(pl.multiple_of(t * 256 + 1024, 256), 256)
            kv[start : start + rows, cols] = dot(
                ext[start : start + rows, :], w_qkv[:, from_cols]
            ).astype(BF16)

    project(288, 576)
    for copy in second:
        copy.wait()
    project(0, 288)
    project(864, 288)

    lane_head = lax.broadcasted_iota(jnp.int32, (96, 256), 1) // 64
    picks = [lane_head == h for h in range(4)]
    nothing = jnp.zeros((96, 256), BF16)
    factor = math.log2(math.e) / 8.0

    def side_copies(t):
        return (
            copy_to(side_out.at[t, 0], side_in.at[t, 1], 4 + 4 * t, west),
            copy_to(side_out.at[t, 1], side_in.at[t, 0], 5 + 4 * t, east),
        )

    def piece_copies(t):
        return (
            copy_to(piece_out.at[t, part(0, 144)], piece_in.at[t, part(144, 144)], 6 + 4 * t, north),
            copy_to(piece_out.at[t, part(144, 144)], piece_in.at[t, part(0, 144)], 7 + 4 * t, south),
        )

    def joined(out):
        total = jnp.where(picks[0], out[0:96], 0.0)
        for h in range(1, 4):
            total = jnp.where(picks[h], out[h * 96 : h * 96 + 96], total)
        return total

    def quad(t):
        cols = pl.ds(pl.multiple_of(t * 256, 256), 256)
        vcols = pl.ds(pl.multiple_of(t * 256 + 1024, 256), 256)
        acc[t] = jnp.zeros((1152, 512), F32)

        @pl.loop(0, 3)
        def _(j):
            rows = pl.ds(pl.multiple_of(j * 96, 96), 96)
            keys = pl.ds(pl.multiple_of(j * 192, 192), 768)
            qj, dj = q[rows, cols], d[rows, cols]
            qm = jnp.concatenate([jnp.where(pick, qj, nothing) for pick in picks], axis=0)
            dm = jnp.concatenate([jnp.where(pick, dj, nothing) for pick in picks], axis=0)
            kw, vw = kv[keys, cols], kv[keys, vcols]
            s = dot_nt(qm, kw).reshape(4, 96, 768) + bias[...][None]
            top = jnp.max(s, axis=-1, keepdims=True)
            e = jnp.exp2((s - top) * factor)
            p = e * (1.0 / jnp.sum(e, axis=-1, keepdims=True))
            p = p.reshape(384, 768)
            pb = p.astype(BF16)
            out = dot(pb, vw)
            delta = jnp.sum(out * dm.astype(F32), axis=-1, keepdims=True)
            ctx[rows, cols] = joined(out).astype(BF16)
            ds = (p * (dot_nt(dm, vw) - delta)).astype(BF16)
            dqkv[rows, cols] = (joined(dot(ds, kw)) * 0.125).astype(BF16)
            acc[t, keys, 0:256] += dot_tn(ds, qm)
            acc[t, keys, 256:512] += dot_tn(pb, dm)

        side_out[t, 0] = acc[t, 0:288, :].astype(BF16)
        side_out[t, 1] = acc[t, 864:1152, :].astype(BF16)
        for copy in side_copies(t):
            copy.start()

    def sides_back(t):
        for copy in side_copies(t):
            copy.wait()
        mid = acc[t, 288:864, :] + side_in[t].astype(F32).reshape(576, 512)
        high = mid.astype(BF16)
        low = (mid - high.astype(F32)).astype(BF16)
        parts = dot(from_middle[...], high)
        piece_out[t, 0:144, :] = parts[0:144].astype(BF16)
        piece_out[t, 144:288, :] = parts[432:576].astype(BF16)
        for copy in piece_copies(t):
            copy.start()
        own[t] = parts[144:432] + dot(from_middle[144:432, :], low)

    def pieces_back(t):
        for copy in piece_copies(t):
            copy.wait()
        total = own[t] + dot(from_piece[...], piece_in[t])
        kcols = pl.ds(pl.multiple_of(t * 256 + 1024, 256), 256)
        vcols = pl.ds(pl.multiple_of(t * 256 + 2048, 256), 256)
        dqkv[:, kcols] = (total[:, 0:256] * 0.125).astype(BF16)
        dqkv[:, vcols] = total[:, 256:512].astype(BF16)

    @pl.loop(0, 6)
    def _(t):
        @pl.when(t < 4)
        def _():
            quad(t)

        @pl.when((t >= 1) & (t < 5))
        def _():
            sides_back(t - 1)

        @pl.when(t >= 2)
        def _():
            pieces_back(t - 2)


def attention(xm, g, w_qkv, w_out, bias):
    order, middle = one_hot(piece_order()), one_hot(middle_order())
    vmem = pl.BlockSpec(memory_space=pltpu.VMEM)
    consts = [jnp.asarray(m, BF16) for m in (order, order.T, middle, middle.T)]
    return pl.pallas_call(
        attention_kernel,
        out_shape=(
            jax.ShapeDtypeStruct((288, 1024), BF16),
            jax.ShapeDtypeStruct((288, 3072), BF16),
        ),
        in_specs=[vmem] * 9,
        out_specs=(vmem,) * 2,
        scratch_shapes=[
            pltpu.VMEM((288, 1024), BF16),
            pltpu.VMEM((576, 1024), BF16),
            pltpu.VMEM((1152, 1024), BF16),
            pltpu.VMEM((288, 1024), BF16),
            pltpu.VMEM((288, 1024), BF16),
            pltpu.VMEM((1152, 2048), BF16),
            pltpu.VMEM((4, 1152, 512), F32),
            pltpu.VMEM((4, 2, 288, 512), BF16),
            pltpu.VMEM((4, 2, 288, 512), BF16),
            pltpu.VMEM((4, 288, 512), BF16),
            pltpu.VMEM((4, 288, 512), BF16),
            pltpu.VMEM((4, 288, 512), F32),
            pltpu.SemaphoreType.DMA((20,)),
            pltpu.SemaphoreType.DMA((20,)),
        ],
        compiler_params=pltpu.CompilerParams(
            collective_id=2, has_side_effects=True, vmem_limit_bytes=60 * 1024 * 1024
        ),
        name="attention",
    )(xm, g, w_qkv, w_out, bias, *consts)


HALF = 2048
WIDE = HALF + 128
PARTS = ((0, 768), (768, 640), (1408, 768))
ORDERS = (("z", "y", "x"), ("x", "z", "y"), ("y", "x", "z"))
REMAINS = (
    ((2, 2, 4), (2, 2), ()),
    ((4, 4), (4,), ()),
    ((4, 2, 2), (4,), ()),
)


def piece_of(part, stage, at):
    every = slice(None)
    hi, lo = lax.div(at, 2), lax.rem(at, 2)
    table = (
        ((at,), (every, every, at), (lo, hi)),
        ((every, lo, hi), (at,), (at,)),
        ((every, every, every, at), (every, lo, hi), (at,)),
    )
    return table[part][stage]


def reduce_kernel(
    lt, rhs, mask_col, gq, go, gm,
    own, got, r10, r11, r12, b0, b1, b2, r20, r21, r22, c0, c1, c2, r30, r31, r32,
    final, crossed, send0, recv0, send, recv, send4, recv4,
):
    r1, r2, r3 = (r10, r11, r12), (r20, r21, r22), (r30, r31, r32)
    sums = (b0, b1, b2), (c0, c1, c2)
    lat, lon = lax.axis_index("lat"), lax.axis_index("lon")
    z, xl = lax.div(lat, 2), lax.rem(lat, 2)
    xh, y, core = lax.div(lon, 8), lax.rem(lax.div(lon, 2), 4), lax.rem(lon, 2)
    x = xh * 2 + xl
    mine = {"x": x, "y": y, "z": z}

    def device(axis, by):
        zz, yy, xx = z, y, x
        if axis == "z":
            zz = lax.rem(z + by, 4)
        elif axis == "y":
            yy = lax.rem(y + by, 4)
        else:
            xx = lax.rem(x + by, 4)
        return (zz * 2 + lax.rem(xx, 2), lax.div(xx, 2) * 8 + yy * 2 + core)

    partner = (lat, lon + 1 - 2 * core)

    barrier = pltpu.get_barrier_semaphore()
    pl.semaphore_signal(barrier, inc=1, device_id=partner, device_id_type=MESH)
    for axis in "xyz":
        for by in (1, 2, 3):
            pl.semaphore_signal(barrier, inc=1, device_id=device(axis, by), device_id_type=MESH)
    pl.semaphore_wait(barrier, 10)

    def make_half(half):
        own[half, :, :, :, :, :, HALF:] = mask_col[...].reshape(4, 2, 2, 4, 16, 128)
        for j in range(2):
            which = half * 2 + j
            left = lax.div(which, 3)

            @pl.loop(0, 4)
            def _(tile):
                rows = pl.ds(pl.multiple_of(tile * 256, 256), 256)
                made = jnp.dot(lt[left, rows, :], rhs[which], preferred_element_type=F32)
                own[half, tile, :, :, :, :, j * 1024 : (j + 1) * 1024] = made.astype(BF16).reshape(
                    2, 2, 4, 16, 1024
                )

    def columns(part):
        return pl.ds(PARTS[part][0], PARTS[part][1])

    make_half(1 - core)
    cross = []
    for part in range(3):
        copy = pltpu.make_async_remote_copy(
            src_ref=own.at[1 - core, :, :, :, :, :, columns(part)],
            dst_ref=got.at[:, :, :, :, :, columns(part)],
            send_sem=send0.at[part],
            recv_sem=recv0.at[part],
            device_id=partner,
            device_id_type=MESH,
        )
        copy.start()
        cross.append(copy)
    make_half(core)

    def start_stage(part, stage, source, slots):
        axis = ORDERS[part][stage]
        copies = []
        for by in (2, 1, 3):
            there = piece_of(part, stage, lax.rem(mine[axis] + by, 4))
            copy = pltpu.make_async_remote_copy(
                src_ref=source(there),
                dst_ref=slots.at[by - 1],
                send_sem=send.at[part * 9 + stage * 3 + by - 1],
                recv_sem=recv.at[part * 9 + stage * 3 + by - 1],
                device_id=device(axis, by),
                device_id_type=MESH,
            )
            copy.start()
            copies.append(copy)
        return copies

    started = []
    for part in range(3):
        cross[part].wait()
        cols = columns(part)

        @pl.loop(0, 4)
        def _(a):
            for b in range(2):
                for c in range(2):
                    total = own[core, a, b, c, :, :, cols].astype(F32) + got[
                        a, b, c, :, :, cols
                    ].astype(F32)
                    own[core, a, b, c, :, :, cols] = total.astype(BF16)

        started.append(
            start_stage(
                part, 0, lambda there, cols=cols: own.at[(core, *there, *open_dims(there, 4), slice(None), cols)], r1[part]
            )
        )
    for part in range(3):
        for copy in started[part]:
            copy.wait()
        cols = columns(part)
        here = piece_of(part, 0, mine[ORDERS[part][0]])
        piece = own[(core, *here, *open_dims(here, 4), slice(None), cols)].astype(F32)
        for slot in range(3):
            piece = piece + r1[part][slot].astype(F32)
        b = sums[0][part]
        b[...] = piece.astype(BF16)
        dims = len(REMAINS[part][0])
        started[part] = start_stage(
            part, 1, lambda there, b=b, dims=dims: b.at[(*there, *open_dims(there, dims))], r2[part]
        )
    for part in range(3):
        for copy in started[part]:
            copy.wait()
        b, c = sums[0][part], sums[1][part]
        dims = len(REMAINS[part][0])
        here = piece_of(part, 1, mine[ORDERS[part][1]])
        piece = b[(*here, *open_dims(here, dims))].astype(F32)
        for slot in range(3):
            piece = piece + r2[part][slot].astype(F32)
        c[...] = piece.astype(BF16)
        started[part] = start_stage(part, 2, lambda there, c=c: c.at[there], r3[part])
    scale = 1.0 / 192.0
    for part in range(3):
        for copy in started[part]:
            copy.wait()
        c = sums[1][part]
        here = piece_of(part, 2, mine[ORDERS[part][2]])
        piece = c[here].astype(F32)
        for slot in range(3):
            piece = piece + r3[part][slot].astype(F32)
        final[:, columns(part)] = piece * scale
    swap = pltpu.make_async_remote_copy(
        src_ref=final.at[pl.ds(pl.multiple_of((1 - core) * 8, 8), 8), pl.ds(0, HALF)],
        dst_ref=crossed,
        send_sem=send4,
        recv_sem=recv4,
        device_id=partner,
        device_id_type=MESH,
    )
    swap.start()
    swap.wait()
    rows = pl.ds(pl.multiple_of(core * 8, 8), 8)
    gm[...] = final[rows, HALF:]

    @pl.when(core == 0)
    def _():
        gq[:, :HALF] = final[rows, :HALF]
        gq[:, HALF:] = crossed[:, :1024]
        go[...] = crossed[:, 1024:]

    @pl.when(core == 1)
    def _():
        gq[:, :HALF] = crossed[...]
        gq[:, HALF:] = final[rows, :1024]
        go[...] = final[rows, 1024:HALF]


def open_dims(there, dims):
    return (slice(None),) * (dims - len(there))


def reduced_gradients(lt, rhs, mask_col):
    stages = [[], [], [], [], []]
    for part, (_, wide) in enumerate(PARTS):
        first, second, _ = REMAINS[part]
        stages[0].append(pltpu.VMEM((3, *first, 16, wide), BF16))
        stages[1].append(pltpu.VMEM((*first, 16, wide), BF16))
        stages[2].append(pltpu.VMEM((3, *second, 16, wide), BF16))
        stages[3].append(pltpu.VMEM((*second, 16, wide), BF16))
        stages[4].append(pltpu.VMEM((3, 16, wide), BF16))
    vmem = pl.BlockSpec(memory_space=pltpu.VMEM)
    return pl.pallas_call(
        reduce_kernel,
        out_shape=(
            jax.ShapeDtypeStruct((8, 3072), F32),
            jax.ShapeDtypeStruct((8, 1024), F32),
            jax.ShapeDtypeStruct((8, 128), F32),
        ),
        in_specs=[vmem] * 3,
        out_specs=(vmem,) * 3,
        scratch_shapes=[
            pltpu.VMEM((2, 4, 2, 2, 4, 16, WIDE), BF16),
            pltpu.VMEM((4, 2, 2, 4, 16, WIDE), BF16),
            *[one for group in stages for one in group],
            pltpu.VMEM((16, WIDE), F32),
            pltpu.VMEM((8, HALF), F32),
            pltpu.SemaphoreType.DMA((3,)),
            pltpu.SemaphoreType.DMA((3,)),
            pltpu.SemaphoreType.DMA((27,)),
            pltpu.SemaphoreType.DMA((27,)),
            pltpu.SemaphoreType.DMA,
            pltpu.SemaphoreType.DMA,
        ],
        compiler_params=pltpu.CompilerParams(
            collective_id=1, has_side_effects=True, vmem_limit_bytes=56 * 1024 * 1024
        ),
        name="reduce_gradients",
    )(lt, rhs, mask_col)


def local(tokens, masked, mask_embed, w_qkv, w_out, cotangent):
    width = tokens.shape[-1]
    hit = jnp.any(masked[0, 0, None, :] == jnp.arange(288, dtype=jnp.int32)[:, None], axis=-1)
    hit = hit.reshape(2, 12, 12).transpose(2, 1, 0).reshape(288, 1)

    def to_own(array):
        return array.transpose(2, 1, 0, 3).reshape(288, width)

    def from_own(array):
        return array.reshape(12, 12, 2, width).transpose(2, 1, 0, 3)

    xm = jnp.where(hit, mask_embed[None, :], to_own(tokens))
    g = to_own(cotangent)
    rows = lax.axis_index("lat") * 12 + jnp.arange(768, dtype=jnp.int32) % 48 // 2 - 6
    on_grid = (rows >= 0) & (rows < 96)
    bias = jnp.where(jnp.asarray(near()) & on_grid[None], 0.0, -jnp.inf).astype(F32)
    ctx, dqkv = attention(xm, g, w_qkv, w_out, bias)
    block_out = (xm.astype(F32) + dot(ctx, w_out)).astype(BF16)
    total = g.astype(F32) + dot_nt(dqkv, w_qkv)
    grad_tokens = jnp.where(hit, 0.0, total).astype(BF16)
    mask_term = jnp.sum(jnp.where(hit, total, 0.0), axis=0)
    lt = jnp.stack([xm.T, ctx.T])
    rhs = jnp.stack([dqkv[:, :width], dqkv[:, width : 2 * width], dqkv[:, 2 * width :], g])
    mask_col = jnp.broadcast_to(mask_term[:, None], (width, 128)).astype(BF16)
    grad_qkv, grad_out, grad_mask = reduced_gradients(lt, rhs, mask_col)
    return (from_own(block_out), from_own(grad_tokens), grad_qkv, grad_out, grad_mask[:, 0])


def solution(mesh):
    placed = (
        P(None, "lat", "lon", None),
        P("lat", "lon", None),
        P(),
        P(),
        P(),
        P(None, "lat", "lon", None),
    )
    return jax.shard_map(
        local,
        mesh=mesh,
        in_specs=placed,
        out_specs=(
            P(None, "lat", "lon", None),
            P(None, "lat", "lon", None),
            P(("lat", "lon"), None),
            P(("lat", "lon"), None),
            P(("lat", "lon")),
        ),
        check_vma=False,
    )
```

profile of v0, /device:TPU:1, one launch (start us, length us, event | category | flops | bytes accessed | tf_op | source)
XLA Modules:
  0.0 178.0 jit_solution(590447294641287689)
XLA Ops:
  0.6 0.8 fusion
  1.4 0.1 reshape.59
  1.5 0.2 copy.67
  1.8 0.2 broadcast_in_dim.53
  1.9 1.7 and_select_fusion.bias
  3.6 0.0 copy-start.4
  3.6 1.6 copy.70
  5.2 0.2 reshape.61.g
  5.5 0.0 copy-start
  5.5 0.2 stack_reshape.3
  5.7 0.0 copy-done.4
  5.7 0.0 copy-start.5
  5.7 0.5 copy.68
  6.2 0.2 reshape.60
  6.5 0.4 copy.69
  6.8 0.0 copy-done.5
  6.8 0.2 broadcast_select_fusion
  7.0 0.2 fusion.13
  7.3 1.1 copy.71.xm
  8.3 0.0 copy-done
  8.3 0.4 copy.74
  8.7 86.8 %attention.1 = (bf16[288,1024]{1,0:T(8,128)(2,1)}, bf16[288,3072]{1,0:T(8,128)(2,1)}) custom-call(bf16[288,1024]{1,0:T(8,128)(2,1)} %copy.71.xm, bf16[288,1024]{1,0:T(8,128)(2,1)} %copy-done, bf16[1024,3072]{1,0:T(8,128)(2,1)} %w_qkv.1, bf16[1024,1024]{1,0:T(8,128)(2,1)} %w_out.1, f32[96,768]{1,0:T(8,128)} %and_select_fusion.bias, ...), custom_call_target="tpu_custom_call" | custom-call | tf_op jit(solution)/shard_map/attention/pallas_call | solution.py:220
  95.5 4.0 %add_convert_fusion = bf16[288,1024]{0,1:T(8,128)(2,1)} fusion(bf16[288,1024]{0,1:T(8,128)(2,1)S(1)} %broadcast_select_fusion, bf16[288,1024]{1,0:T(8,128)(2,1)} %get-tuple-element.10, bf16[1024,1024]{1,0:T(8,128)(2,1)} %w_out.1), kind=kOutput, calls=%fused_computation.5 | convolution fusion | flops 604864512 | bytes 3866624 | tf_op jit(solution)/shard_map/dot_general | solution.py:45
  99.5 1.4 copy.73
  100.9 0.2 reshape.62
  101.1 1.3 copy.79
  102.5 1.4 copy.77
  103.9 0.0 copy-start.1
  103.9 1.5 pad_maximum_fusion.1.lt
  105.4 0.5 copy-done.1
  105.9 7.7 %select_convert_fusion = (bf16[288,1024]{0,1:T(8,128)(2,1)}, f32[288,1024]{0,1:T(8,128)}) fusion(pred[288]{0:T(512)(128)(4,1)S(1)} %broadcast_in_dim.53, bf16[288,3072]{1,0:T(8,128)(2,1)S(1)} %copy-done.1, bf16[1024,3072]{1,0:T(8,128)(2,1)} %w_qkv.1, bf16[288,1024]{0,1:T(8,128)(2,1)S(1)} %copy.74), kind=kOutput, calls=%fused_computation.3 | convolution fusion | flops 1812824064 | bytes 10420512 | tf_op jit(solution)/shard_map/dot_general | solution.py:49
  113.5 0.0 copy-start.2
  113.5 1.5 copy.76
  115.0 0.2 reshape.63
  115.3 1.3 copy.80
  116.6 0.0 copy-done.2
  116.6 0.1 slice_bitcast_fusion.2
  116.8 0.0 copy-start.3
  116.8 1.7 pad_maximum_fusion.rhs
  118.5 0.1 copy-done.3
  118.6 0.2 select_reduce_fusion
  118.8 0.9 broadcast_in_dim.59.mask_col
  119.7 54.1 %reduce_gradients.1 = (f32[8,3072]{1,0:T(8,128)}, f32[8,1024]{1,0:T(8,128)}, f32[8,128]{1,0:T(8,128)}) custom-call(bf16[2,1024,288]{2,1,0:T(8,128)(2,1)} %pad_maximum_fusion.1.lt, bf16[4,288,1024]{2,1,0:T(8,128)(2,1)} %pad_maximum_fusion.rhs, bf16[1024,128]{1,0:T(8,128)(2,1)} %broadcast_in_dim.59.mask_col), custom_call_target="tpu_custom_call" | custom-call | tf_op jit(solution)/shard_map/reduce_gradients/pallas_call | solution.py:448
  173.8 1.3 slice_reduce_fusion
  175.1 1.5 copy.86
  176.6 1.4 copy.87
  (1 shorter events, 0.0 us)
Async XLA Ops:
  3.6 2.1 %copy-start.4 = (bf16[2,12,12,1024]{3,0,2,1:T(2,128)(2,1)S(1)}, bf16[2,12,12,1024]{3,0,2,1:T(2,128)(2,1)}, u32[]{:S(2)}) copy-start(bf16[2,12,12,1024]{3,0,2,1:T(2,128)(2,1)} %param.11) | copy-start | bytes 1769476
  5.5 2.9 %copy-start = (bf16[288,1024]{1,0:T(8,128)(2,1)}, bf16[288,1024]{1,0:T(8,128)(2,1)S(1)}, u32[]{:S(2)}) copy-start(bf16[288,1024]{1,0:T(8,128)(2,1)S(1)} %reshape.61.g) | copy-start | bytes 1769476
  5.7 1.1 copy-start.5
  103.9 2.0 %copy-start.1 = (bf16[288,3072]{1,0:T(8,128)(2,1)S(1)}, bf16[288,3072]{1,0:T(8,128)(2,1)}, u32[]{:S(2)}) copy-start(bf16[288,3072]{1,0:T(8,128)(2,1)} %get-tuple-element.11) | copy-start | bytes 5308420
  113.5 3.1 %copy-start.2 = (bf16[288,3072]{1,0:T(8,128)(2,1)S(1)}, bf16[288,3072]{1,0:T(8,128)(2,1)}, u32[]{:S(2)}) copy-start(bf16[288,3072]{1,0:T(8,128)(2,1)} %get-tuple-element.11) | copy-start | bytes 5308420
  116.8 1.8 %copy-start.3 = (f32[288,1024]{0,1:T(8,128)S(1)}, f32[288,1024]{0,1:T(8,128)}, u32[]{:S(2)}) copy-start(f32[288,1024]{0,1:T(8,128)} %get-tuple-element.39) | copy-start | bytes 3538948
where the time goes:
time: 179 us; the launch traced here: 178 us
  Pallas kernels  141 us (79%)
  local copies, waits for them, and re-layouts  18.4 us (10%)
  matrix products  11.6 us (6%)
  other arithmetic  6.25 us (3%)
    pallas_call x1, Pallas kernels, attention(): pl.pallas_call(attention_kernel, out_shape=(jax.ShapeDtypeStruct((288, 10...  86.8 us
    pallas_call x1, Pallas kernels, reduced_gradients(): pl.pallas_call(reduce_kernel, out_shape=(jax.ShapeDtypeStruct((8, 3072),...  54.1 us
    dot_general x1, matrix products, dot_nt(): lax.dot_general(a, b, (((1,), (1,)), ((), ())), preferred_element_type=F32)  7.65 us
    unnamed x16, local copies, waits for them, and re-layouts  6.2 us
    dot_general x1, matrix products, dot(): return jnp.dot(a, b, preferred_element_type=F32)  3.99 us

commit v1 on v0

v1 whole, which is shorter than its diff:
```python
import math

import jax
import jax.numpy as jnp
import numpy as np
from jax import lax
from jax.experimental import pallas as pl
from jax.experimental.pallas import tpu as pltpu
from jax.sharding import PartitionSpec as P

HEADS = 16
MESH = pl.DeviceIdType.MESH
BF16 = jnp.bfloat16
F32 = jnp.float32
EVERY = slice(None)


JOBS = (
    (0, 0, 512, "zyx"),
    (0, 512, 512, "yzx"),
    (1, 0, 384, "xzy"),
    (1, 384, 384, "zyx"),
    (1, 768, 384, "yxz"),
)
WIDE = (1024, 1152)


def piece_order():
    column, row, lev = np.meshgrid(np.arange(12), np.arange(6), np.arange(2), indexing="ij")
    top = (column * 24 + row * 2 + lev).reshape(-1)
    return np.concatenate([top, top + 12])


def middle_order():
    column, row, lev = np.meshgrid(np.arange(12), np.arange(24), np.arange(2), indexing="ij")
    north = column * 12 + row * 2 + lev
    inside = 144 + column * 24 + (row - 6) * 2 + lev
    south = 432 + column * 12 + (row - 18) * 2 + lev
    return np.where(row < 6, north, np.where(row < 18, inside, south)).reshape(-1)


def padded_order():
    column, row, lev = np.meshgrid(np.arange(12), np.arange(12), np.arange(2), indexing="ij")
    return (lev * 192 + row * 16 + column).reshape(-1)


def one_hot(order, size):
    return (order[:, None] == np.arange(size)[None, :]).astype(np.float32)


def near():
    query = np.arange(96)
    key = np.arange(768)
    row, column = query % 24 // 2, query // 24
    krow, kcolumn = key % 48 // 2, key // 48
    allowed = (krow[None] >= row[:, None]) & (krow[None] <= row[:, None] + 11)
    return allowed & (kcolumn[None] >= column[:, None]) & (kcolumn[None] <= column[:, None] + 11)


def dot(a, b):
    return jnp.dot(a, b, preferred_element_type=F32)


def dot_nt(a, b):
    return lax.dot_general(a, b, (((1,), (1,)), ((), ())), preferred_element_type=F32)


def dot_tn(a, b):
    return lax.dot_general(a, b, (((0,), (0,)), ((), ())), preferred_element_type=F32)


def without(axes, count):
    return [axis for axis in "zxy" if axis not in axes[:count]]


def extent(axes):
    return tuple(size for axis in axes for size in ((2, 2) if axis == "x" else (4,)))


def index_of(axes, chosen, at):
    out = []
    for axis in axes:
        if axis == "x":
            out += [lax.rem(at, 2), lax.div(at, 2)] if chosen == "x" else [EVERY, EVERY]
        else:
            out += [at] if axis == chosen else [EVERY]
    return tuple(out)


def block_kernel(
    tokens, masked, embed, w_qkv_hbm, w_out_hbm, cotangent, near_bias,
    from_padded, to_padded, to_piece, from_piece, to_middle, from_middle,
    block_out, grad_tokens, gq, go, gm,
    w_qkv, w_out, padded, xm, g, bias, hits, ctx, dqkv,
    pieces, stacked, ext, q, d, kv, acc, side_out, side_in, piece_out, piece_in, own_kv,
    made, got_a, got_b, *rest,
):
    scratch = [rest[5 * i : 5 * i + 5] for i in range(5)]
    final_a, final_b, cross_a, cross_b, load, send, recv = rest[25:]
    lat, lon = lax.axis_index("lat"), lax.axis_index("lon")
    z, xl = lax.div(lat, 2), lax.rem(lat, 2)
    xh, y, core = lax.div(lon, 8), lax.rem(lax.div(lon, 2), 4), lax.rem(lon, 2)
    x = xh * 2 + xl
    mine = {"x": x, "y": y, "z": z}

    def device(axis, by):
        zz, yy, xx = z, y, x
        if axis == "z":
            zz = lax.rem(z + by, 4)
        elif axis == "y":
            yy = lax.rem(y + by, 4)
        else:
            xx = lax.rem(x + by, 4)
        return (zz * 2 + lax.rem(xx, 2), lax.div(xx, 2) * 8 + yy * 2 + core)

    partner = (lat, lon + 1 - 2 * core)
    north, south = (lax.rem(lat + 7, 8), lon), (lax.rem(lat + 1, 8), lon)
    west, east = (lat, lax.rem(lon + 15, 16)), (lat, lax.rem(lon + 1, 16))

    barrier = pltpu.get_barrier_semaphore()
    greeted = [north, south, west, east, partner]
    greeted += [device(axis, by) for axis in "xyz" for by in (1, 2, 3)]
    for other in greeted:
        pl.semaphore_signal(barrier, inc=1, device_id=other, device_id_type=MESH)

    loads = (
        pltpu.make_async_copy(w_qkv_hbm, w_qkv, load.at[0]),
        pltpu.make_async_copy(w_out_hbm, w_out, load.at[1]),
    )
    for copy in loads:
        copy.start()

    place = lax.broadcasted_iota(jnp.int32, (288, 144), 0)
    place = lax.rem(place, 2) * 144 + lax.div(lax.rem(place, 24), 2) * 12 + lax.div(place, 24)
    found = jnp.where(masked[0] == place, 1.0, 0.0)
    hit = jnp.max(found, axis=-1, keepdims=True) > 0.5
    hits[...] = jnp.where(hit, 1.0, 0.0) + jnp.zeros((288, 128), F32)
    padded[...] = jnp.zeros((24, 16, 1024), BF16)
    padded[:, 0:12, :] = tokens[...].reshape(24, 12, 1024)
    own_tokens = dot(from_padded[...], padded[...].reshape(384, 1024))
    xm[...] = jnp.where(hit, embed[...].astype(F32), own_tokens).astype(BF16)

    pieces[...] = dot(to_piece[...], xm[...]).astype(BF16)
    stacked[144:432, :] = xm[...]
    pl.semaphore_wait(barrier, len(greeted))

    def copy_to(source, target, sem, other):
        return pltpu.make_async_remote_copy(
            src_ref=source,
            dst_ref=target,
            send_sem=send.at[sem],
            recv_sem=recv.at[sem],
            device_id=other,
            device_id_type=MESH,
        )

    def part(start, rows):
        return pl.ds(start, rows)

    def tile(t, start=0):
        return pl.ds(pl.multiple_of(t * 256 + start, 256), 256)

    first = (
        copy_to(pieces.at[part(0, 144)], stacked.at[part(432, 144)], 0, north),
        copy_to(pieces.at[part(144, 144)], stacked.at[part(0, 144)], 1, south),
    )
    for copy in first:
        copy.start()

    padded[:, 0:12, :] = cotangent[...].reshape(24, 12, 1024)
    g[...] = dot(from_padded[...], padded[...].reshape(384, 1024)).astype(BF16)
    key_row = lax.broadcasted_iota(jnp.int32, (1, 768), 1)
    key_row = lax.div(lax.rem(key_row, 48), 2) + lat * 12 - 6
    bias[...] = jnp.where((key_row >= 0) & (key_row < 96), near_bias[...], -jnp.inf)
    for copy in loads:
        copy.wait()

    @pl.loop(0, 4)
    def _(t):
        cols = tile(t)
        q[:, cols] = dot(xm[...], w_qkv[:, cols]).astype(BF16)
        d[:, cols] = dot_nt(g[...], w_out[cols, :]).astype(BF16)

    for copy in first:
        copy.wait()
    ext[288:864, :] = dot(to_middle[...], stacked[...]).astype(BF16)
    second = (
        copy_to(ext.at[part(288, 288)], ext.at[part(864, 288)], 2, west),
        copy_to(ext.at[part(576, 288)], ext.at[part(0, 288)], 3, east),
    )
    for copy in second:
        copy.start()

    def project(start, rows):
        @pl.loop(0, 8)
        def _(t):
            kv[start : start + rows, tile(t)] = dot(
                ext[start : start + rows, :], w_qkv[:, tile(t, 1024)]
            ).astype(BF16)

    project(288, 576)
    for copy in second:
        copy.wait()
    project(0, 288)
    project(864, 288)

    lane_head = lax.div(lax.broadcasted_iota(jnp.int32, (96, 256), 1), 64)
    picks = [lane_head == h for h in range(4)]
    nothing = jnp.zeros((96, 256), BF16)
    factor = math.log2(math.e) / 8.0

    def side_copies(t):
        return (
            copy_to(side_out.at[t, 0], side_in.at[t, 1], 4 + 4 * t, west),
            copy_to(side_out.at[t, 1], side_in.at[t, 0], 5 + 4 * t, east),
        )

    def piece_copies(t):
        return (
            copy_to(piece_out.at[t, part(0, 144)], piece_in.at[t, part(144, 144)], 6 + 4 * t, north),
            copy_to(piece_out.at[t, part(144, 144)], piece_in.at[t, part(0, 144)], 7 + 4 * t, south),
        )

    def joined(out):
        total = jnp.where(picks[0], out[0:96], 0.0)
        for h in range(1, 4):
            total = jnp.where(picks[h], out[h * 96 : h * 96 + 96], total)
        return total

    def quad(t):
        cols, vcols = tile(t), tile(t, 1024)
        slot = lax.rem(t, 2)
        acc[slot] = jnp.zeros((1152, 512), F32)

        @pl.loop(0, 3)
        def _(j):
            rows = pl.ds(pl.multiple_of(j * 96, 96), 96)
            keys = pl.ds(pl.multiple_of(j * 192, 192), 768)
            qj, dj = q[rows, cols], d[rows, cols]
            qm = jnp.concatenate([jnp.where(pick, qj, nothing) for pick in picks], axis=0)
            dm = jnp.concatenate([jnp.where(pick, dj, nothing) for pick in picks], axis=0)
            kw, vw = kv[keys, cols], kv[keys, vcols]
            s = dot_nt(qm, kw).reshape(4, 96, 768) + bias[...][None]
            top = jnp.max(s, axis=-1, keepdims=True)
            e = jnp.exp2((s - top) * factor)
            p = e * (1.0 / jnp.sum(e, axis=-1, keepdims=True))
            p = p.reshape(384, 768)
            pb = p.astype(BF16)
            out = dot(pb, vw)
            delta = jnp.sum(out * dm.astype(F32), axis=-1, keepdims=True)
            ctx[rows, cols] = joined(out).astype(BF16)
            ds = (p * (dot_nt(dm, vw) - delta)).astype(BF16)
            dqkv[rows, cols] = (joined(dot(ds, kw)) * 0.125).astype(BF16)
            acc[slot, keys, 0:256] += dot_tn(ds, qm)
            acc[slot, keys, 256:512] += dot_tn(pb, dm)

        side_out[t, 0] = acc[slot, 0:288, :].astype(BF16)
        side_out[t, 1] = acc[slot, 864:1152, :].astype(BF16)
        for copy in side_copies(t):
            copy.start()

    def sides_back(t):
        for copy in side_copies(t):
            copy.wait()
        slot = lax.rem(t, 2)
        mid = acc[slot, 288:864, :] + side_in[t].astype(F32).reshape(576, 512)
        high = mid.astype(BF16)
        low = (mid - high.astype(F32)).astype(BF16)
        parts = dot(from_middle[...], high)
        piece_out[t, 0:144, :] = parts[0:144].astype(BF16)
        piece_out[t, 144:288, :] = parts[432:576].astype(BF16)
        for copy in piece_copies(t):
            copy.start()
        own_kv[slot] = parts[144:432] + dot(from_middle[144:432, :], low)

    def pieces_back(t):
        for copy in piece_copies(t):
            copy.wait()
        total = own_kv[lax.rem(t, 2)] + dot(from_piece[...], piece_in[t])
        dqkv[:, tile(t, 1024)] = (total[:, 0:256] * 0.125).astype(BF16)
        dqkv[:, tile(t, 2048)] = total[:, 256:512].astype(BF16)

    @pl.loop(0, 4)
    def _(t):
        quad(t)

        @pl.when(t >= 1)
        def _():
            sides_back(t - 1)

        @pl.when(t >= 2)
        def _():
            pieces_back(t - 2)

    gots = (got_a, got_b)

    def columns(job):
        return pl.ds(JOBS[job][1], JOBS[job][2])

    def store_made(half, t, value):
        made[half, t, :, :, :, :, 0:1024] = value.astype(BF16).reshape(2, 2, 4, 16, 1024)

    def make_a(half):
        @pl.when(half == 0)
        def _():
            @pl.loop(0, 4)
            def _(t):
                store_made(half, t, dot_tn(xm[:, tile(t)], dqkv[:, 0:1024]))

        @pl.when(half == 1)
        def _():
            @pl.loop(0, 4)
            def _(t):
                store_made(half, t, dot_tn(ctx[:, tile(t)], g[...]))

    def make_b(half):
        cols = pl.ds(pl.multiple_of(half * 1024 + 1024, 1024), 1024)

        @pl.loop(0, 4)
        def _(t):
            store_made(half, t, dot_tn(xm[:, tile(t)], dqkv[:, cols]))

    def exchange(job):
        where = (EVERY,) * 5 + (columns(job),)
        return copy_to(made.at[(1 - core, *where)], gots[JOBS[job][0]].at[where], 20 + job, partner)

    def exchanged(job):
        exchange(job).wait()
        cols, got = columns(job), gots[JOBS[job][0]]

        @pl.loop(0, 4)
        def _(a):
            for b in range(2):
                for c in range(2):
                    total = made[core, a, b, c, :, :, cols].astype(F32)
                    total = total + got[a, b, c, :, :, cols].astype(F32)
                    made[core, a, b, c, :, :, cols] = total.astype(BF16)

    def held(job, stage, at):
        order = JOBS[job][3]
        here = index_of(without(order, stage), order[stage], at)
        if stage == 0:
            return made, (core, *here, EVERY, columns(job))
        return scratch[job][2 * stage - 1], (*here, EVERY, EVERY)

    def stage_copies(job, stage):
        axis = JOBS[job][3][stage]
        copies = []
        for by in (2, 1, 3):
            ref, where = held(job, stage, lax.rem(mine[axis] + by, 4))
            target = scratch[job][2 * stage].at[by - 1]
            sem = 25 + job * 9 + stage * 3 + by - 1
            copies.append(copy_to(ref.at[where], target, sem, device(axis, by)))
        return copies

    def start(job, stage):
        for copy in stage_copies(job, stage):
            copy.start()

    def reduced(job, stage):
        for copy in stage_copies(job, stage):
            copy.wait()
        ref, where = held(job, stage, mine[JOBS[job][3][stage]])
        piece = ref[where].astype(F32)
        for slot in range(3):
            piece = piece + scratch[job][2 * stage][slot].astype(F32)
        if stage < 2:
            scratch[job][2 * stage + 1][...] = piece.astype(BF16)
        else:
            final = (final_a, final_b)[JOBS[job][0]]
            final[:, columns(job)] = piece * (1.0 / 192.0)

    def swap(phase):
        rows = pl.ds(pl.multiple_of((1 - core) * 8, 8), 8)
        source = (final_a, final_b)[phase].at[rows, pl.ds(0, 1024)]
        return copy_to(source, (cross_a, cross_b)[phase], 70 + phase, partner)

    make_a(1 - core)
    for job in (0, 1):
        exchange(job).start()
    sides_back(3)
    make_a(core)
    for job in (0, 1):
        exchanged(job)
        start(job, 0)
    pieces_back(2)

    @pl.loop(0, 4)
    def _(t):
        cols = tile(t)
        value = xm[:, cols].astype(F32) + dot(ctx[...], w_out[:, cols])
        value = dot(to_padded[...], value.astype(BF16)).astype(BF16)
        block_out[:, :, :, cols] = value.reshape(2, 12, 16, 256)[:, :, 0:12, :]

    for job in (0, 1):
        reduced(job, 0)
        start(job, 1)
    pieces_back(3)

    make_b(1 - core)
    for job in (2, 3):
        exchange(job).start()

    @pl.loop(0, 4)
    def _(t):
        cols = tile(t)
        hit = hits[...]
        total = g[:, cols].astype(F32) + dot_nt(dqkv[...], w_qkv[cols, :])
        kept = jnp.where(jnp.concatenate([hit, hit], axis=1) > 0.5, 0.0, total).astype(BF16)
        kept = dot(to_padded[...], kept).astype(BF16)
        grad_tokens[:, :, :, cols] = kept.reshape(2, 12, 16, 256)[:, :, 0:12, :]
        high = total.astype(BF16)
        low = (total - high.astype(F32)).astype(BF16)
        column = dot_tn(high, hit.astype(BF16)) + dot_tn(low, hit.astype(BF16))
        column = column.astype(BF16).reshape(2, 2, 4, 16, 128)
        made[0, t, :, :, :, :, 1024:1152] = column
        made[1, t, :, :, :, :, 1024:1152] = column

    exchange(4).start()
    make_b(core)
    for job in (0, 1):
        reduced(job, 1)
        start(job, 2)
    for job in (2, 3, 4):
        exchanged(job)
        start(job, 0)
    for job in (0, 1):
        reduced(job, 2)
    swap(0).start()
    for stage in (0, 1):
        for job in (2, 3, 4):
            reduced(job, stage)
            start(job, stage + 1)
    for job in (2, 3, 4):
        reduced(job, 2)
    swap(1).start()
    swap(0).wait()
    swap(1).wait()
    rows = pl.ds(pl.multiple_of(core * 8, 8), 8)
    gm[...] = final_b[rows, 1024:]

    @pl.when(core == 0)
    def _():
        gq[:, 0:1024] = final_a[rows, :]
        gq[:, 1024:2048] = final_b[rows, 0:1024]
        gq[:, 2048:] = cross_b[...]
        go[...] = cross_a[...]

    @pl.when(core == 1)
    def _():
        gq[:, 0:1024] = cross_a[...]
        gq[:, 1024:2048] = cross_b[...]
        gq[:, 2048:] = final_b[rows, 0:1024]
        go[...] = final_a[rows, :]


def local(tokens, masked, mask_embed, w_qkv, w_out, cotangent):
    natural = one_hot(padded_order(), 384)
    piece, middle = one_hot(piece_order(), 288), one_hot(middle_order(), 576)
    orders = [natural, natural.T, piece, piece.T, middle, middle.T]
    near_bias = np.where(near(), 0.0, -np.inf).astype(np.float32)
    vmem, hbm = pl.BlockSpec(memory_space=pltpu.VMEM), pl.BlockSpec(memory_space=pl.ANY)
    jobs = []
    for _, _, wide, order in JOBS:
        for stage in (1, 2):
            left = extent(without(order, stage))
            jobs.append(pltpu.VMEM((3, *left, 16, wide), BF16))
            jobs.append(pltpu.VMEM((*left, 16, wide), BF16))
        jobs.append(pltpu.VMEM((3, 16, wide), BF16))
    block_out, grad_tokens, gq, go, gm = pl.pallas_call(
        block_kernel,
        out_shape=(
            jax.ShapeDtypeStruct(tokens.shape, BF16),
            jax.ShapeDtypeStruct(tokens.shape, BF16),
            jax.ShapeDtypeStruct((8, 3072), F32),
            jax.ShapeDtypeStruct((8, 1024), F32),
            jax.ShapeDtypeStruct((8, 128), F32),
        ),
        in_specs=[vmem, vmem, vmem, hbm, hbm, vmem, vmem] + [vmem] * 6,
        out_specs=(vmem,) * 5,
        scratch_shapes=[
            pltpu.VMEM((1024, 3072), BF16),
            pltpu.VMEM((1024, 1024), BF16),
            pltpu.VMEM((24, 16, 1024), BF16),
            pltpu.VMEM((288, 1024), BF16),
            pltpu.VMEM((288, 1024), BF16),
            pltpu.VMEM((96, 768), F32),
            pltpu.VMEM((288, 128), F32),
            pltpu.VMEM((288, 1024), BF16),
            pltpu.VMEM((288, 3072), BF16),
            pltpu.VMEM((288, 1024), BF16),
            pltpu.VMEM((576, 1024), BF16),
            pltpu.VMEM((1152, 1024), BF16),
            pltpu.VMEM((288, 1024), BF16),
            pltpu.VMEM((288, 1024), BF16),
            pltpu.VMEM((1152, 2048), BF16),
            pltpu.VMEM((2, 1152, 512), F32),
            pltpu.VMEM((4, 2, 288, 512), BF16),
            pltpu.VMEM((4, 2, 288, 512), BF16),
            pltpu.VMEM((4, 288, 512), BF16),
            pltpu.VMEM((4, 288, 512), BF16),
            pltpu.VMEM((2, 288, 512), F32),
            pltpu.VMEM((2, 4, 2, 2, 4, 16, 1152), BF16),
            pltpu.VMEM((4, 2, 2, 4, 16, 1024), BF16),
            pltpu.VMEM((4, 2, 2, 4, 16, 1152), BF16),
            *jobs,
            pltpu.VMEM((16, 1024), F32),
            pltpu.VMEM((16, 1152), F32),
            pltpu.VMEM((8, 1024), F32),
            pltpu.VMEM((8, 1024), F32),
            pltpu.SemaphoreType.DMA((2,)),
            pltpu.SemaphoreType.DMA((72,)),
            pltpu.SemaphoreType.DMA((72,)),
        ],
        compiler_params=pltpu.CompilerParams(
            collective_id=1, has_side_effects=True, vmem_limit_bytes=62 * 1024 * 1024
        ),
        name="attention_block",
    )(
        tokens, masked, mask_embed[None], w_qkv, w_out, cotangent, jnp.asarray(near_bias),
        *[jnp.asarray(order, BF16) for order in orders],
    )
    return (block_out, grad_tokens, gq, go, gm[:, 0])


def solution(mesh):
    placed = (
        P(None, "lat", "lon", None),
        P("lat", "lon", None),
        P(),
        P(),
        P(),
        P(None, "lat", "lon", None),
    )
    return jax.shard_map(
        local,
        mesh=mesh,
        in_specs=placed,
        out_specs=(
            P(None, "lat", "lon", None),
            P(None, "lat", "lon", None),
            P(("lat", "lon"), None),
            P(("lat", "lon"), None),
            P(("lat", "lon")),
        ),
        check_vma=False,
    )
```

time: 179 us -> 147 us (0.82)
  matrix products: 11.6 us -> 0 us
  Pallas kernels: 141 us -> 131 us
  other arithmetic: 6.25 us -> 0 us
  local copies, waits for them, and re-layouts: 18.4 us -> 14.8 us
    dot_general x2 -> x0, matrix products: 11.6 us -> none  [the longest x1 7.65 us: dot_nt(): lax.dot_general(a, b, (((1,), (1,)), ((), ())), preferred_element_type=F32)]
    pallas_call x2 -> x1, Pallas kernels: 141 us -> 131 us  [local(): pl.pallas_call(block_kernel, out_shape=(jax.ShapeDtypeStruct(tokens.shape...]
    unnamed x16 -> x6, local copies, waits for them, and re-layouts: 6.2 us -> 12.3 us
    another operation x3 -> x0, other arithmetic: 3.38 us -> none  [the longest x1 1.72 us: local(): jnp.stack([dqkv[:, :width], dqkv[:, width:2 * width], dqkv[:, 2 * width:]...]
    convert_element_type x2 -> x0, local copies, waits for them, and re-layouts: 2.89 us -> none  [the longest x1 1.51 us: local(): grad_tokens = jnp.where(hit, 0.0, total).astype(BF16)]
    transpose x3 -> x0, local copies, waits for them, and re-layouts: 2.36 us -> none  [the longest x2 2.13 us: to_own(): return array.transpose(2, 1, 0, 3).reshape(288, width)]
    select_n x2 -> x0, other arithmetic: 1.86 us -> none  [the longest x1 1.65 us: local(): jnp.where(jnp.asarray(near()) & on_grid[None], 0.0, -jnp.inf).astype(F32)]
where the time goes in v1:
time: 147 us
  Pallas kernels  131 us (89%)
  local copies, waits for them, and re-layouts  14.8 us (10%)
    pallas_call x1, Pallas kernels, local(): pl.pallas_call(block_kernel, out_shape=(jax.ShapeDtypeStruct(tokens.shape...  131 us
    unnamed x6, local copies, waits for them, and re-layouts  12.3 us

profile of v1, /device:TPU:1, one launch (start us, length us, event | category | flops | bytes accessed | tf_op | source)
XLA Modules:
  0.0 146.8 jit_solution(16321111156027403342)
XLA Ops:
  0.6 1.3 broadcast_in_dim.3.embed
  1.9 2.1 %copy.22.tokens = bf16[2,12,12,1024]{3,2,1,0:T(8,128)(2,1)} copy(bf16[2,12,12,1024]{3,0,2,1:T(2,128)(2,1)} %param.13) | data formatting | bytes 1179648 | tf_op args[0]
  4.0 2.1 %copy.23.cotangent = bf16[2,12,12,1024]{3,2,1,0:T(8,128)(2,1)} copy(bf16[2,12,12,1024]{3,0,2,1:T(2,128)(2,1)} %param.18) | data formatting | bytes 1179648 | tf_op args[5]
  6.1 131.4 %attention_block.1 = (bf16[2,12,12,1024]{3,2,1,0:T(8,128)(2,1)}, bf16[2,12,12,1024]{3,2,1,0:T(8,128)(2,1)}, f32[8,3072]{1,0:T(8,128)}, f32[8,1024]{1,0:T(8,128)}, f32[8,128]{1,0:T(8,128)}) custom-call(bf16[2,12,12,1024]{3,2,1,0:T(8,128)(2,1)} %copy.22.tokens, s32[1,1,144]{2,1,0:T(1,128)} %masked.1, bf16[1,1024]{1,0:T(2,128)(2,1)} %broadcast_in_dim.3.embed, ...), custom_call_target="tpu_custom_call" | custom-call | tf_op jit(solution)/shard_map/attention_block/pallas_call | solution.py:470
  137.5 2.6 %copy.24 = bf16[2,12,12,1024]{3,0,2,1:T(2,128)(2,1)} copy(bf16[2,12,12,1024]{3,2,1,0:T(8,128)(2,1)} %get-tuple-element.20) | data formatting | bytes 1179648
  140.1 1.3 slice_reduce_fusion
  141.4 2.6 %copy.25 = bf16[2,12,12,1024]{3,0,2,1:T(2,128)(2,1)} copy(bf16[2,12,12,1024]{3,2,1,0:T(8,128)(2,1)} %get-tuple-element.21) | data formatting | bytes 1179648
  143.9 1.5 %copy.28 = f32[8,3072]{1,0:T(8,128)} copy(f32[8,3072]{1,0:T(8,128)} %get-tuple-element.32) | data formatting | bytes 196608
  145.5 1.4 copy.29

commit v2 on v1

--- a/solution.py
+++ b/solution.py
@@ -18,11 +18,15 @@
 JOBS = (
     (0, 0, 512, "zyx"),
     (0, 512, 512, "yzx"),
-    (1, 0, 384, "xzy"),
-    (1, 384, 384, "zyx"),
-    (1, 768, 384, "yxz"),
+    (1, 0, 256, "zyx"),
+    (1, 256, 256, "yzx"),
+    (1, 512, 128, "zyx"),
+    (1, 640, 128, "yzx"),
+    (1, 768, 128, "xzy"),
+    (1, 896, 128, "yxz"),
+    (1, 1024, 128, "zyx"),
 )
-WIDE = (1024, 1152)
+OF_QUAD = ((2,), (3,), (4, 5), (6, 7))
 
 
 def piece_order():
@@ -39,9 +43,9 @@
     return np.where(row < 6, north, np.where(row < 18, inside, south)).reshape(-1)
 
 
-def padded_order():
+def given_order():
     column, row, lev = np.meshgrid(np.arange(12), np.arange(12), np.arange(2), indexing="ij")
-    return (lev * 192 + row * 16 + column).reshape(-1)
+    return (row * 24 + column * 2 + lev).reshape(-1)
 
 
 def one_hot(order, size):
@@ -88,15 +92,15 @@
 
 
 def block_kernel(
-    tokens, masked, embed, w_qkv_hbm, w_out_hbm, cotangent, near_bias,
-    from_padded, to_padded, to_piece, from_piece, to_middle, from_middle,
+    tokens, masked, place, embed, w_qkv_hbm, w_out_hbm, cotangent, near_bias,
+    from_given, to_given, to_piece, from_piece, to_middle, from_middle,
     block_out, grad_tokens, gq, go, gm,
-    w_qkv, w_out, padded, xm, g, bias, hits, ctx, dqkv,
+    w_qkv, w_out, xm, g, bias, hits, ctx, dqkv,
     pieces, stacked, ext, q, d, kv, acc, side_out, side_in, piece_out, piece_in, own_kv,
-    made, got_a, got_b, *rest,
+    total, made_a, made_b, got_a, got_b, *rest,
 ):
-    scratch = [rest[5 * i : 5 * i + 5] for i in range(5)]
-    final_a, final_b, cross_a, cross_b, load, send, recv = rest[25:]
+    scratch = [rest[5 * i : 5 * i + 5] for i in range(len(JOBS))]
+    final_a, final_b, cross_a, cross_b, load, send, recv = rest[5 * len(JOBS) :]
     lat, lon = lax.axis_index("lat"), lax.axis_index("lon")
     z, xl = lax.div(lat, 2), lax.rem(lat, 2)
     xh, y, core = lax.div(lon, 8), lax.rem(lax.div(lon, 2), 4), lax.rem(lon, 2)
@@ -130,15 +134,12 @@
     for copy in loads:
         copy.start()
 
-    place = lax.broadcasted_iota(jnp.int32, (288, 144), 0)
-    place = lax.rem(place, 2) * 144 + lax.div(lax.rem(place, 24), 2) * 12 + lax.div(place, 24)
-    found = jnp.where(masked[0] == place, 1.0, 0.0)
+    found = jnp.where(masked[0] == place[...], 1.0, 0.0)
     hit = jnp.max(found, axis=-1, keepdims=True) > 0.5
     hits[...] = jnp.where(hit, 1.0, 0.0) + jnp.zeros((288, 128), F32)
-    padded[...] = jnp.zeros((24, 16, 1024), BF16)
-    padded[:, 0:12, :] = tokens[...].reshape(24, 12, 1024)
-    own_tokens = dot(from_padded[...], padded[...].reshape(384, 1024))
-    xm[...] = jnp.where(hit, embed[...].astype(F32), own_tokens).astype(BF16)
+    own_tokens = dot(from_given[...], tokens[...].reshape(288, 1024))
+    mask_row = jnp.concatenate([embed[i : i + 1, :] for i in range(8)], axis=1).astype(F32)
+    xm[...] = jnp.where(hit, mask_row, own_tokens).astype(BF16)
 
     pieces[...] = dot(to_piece[...], xm[...]).astype(BF16)
     stacked[144:432, :] = xm[...]
@@ -167,8 +168,7 @@
     for copy in first:
         copy.start()
 
-    padded[:, 0:12, :] = cotangent[...].reshape(24, 12, 1024)
-    g[...] = dot(from_padded[...], padded[...].reshape(384, 1024)).astype(BF16)
+    g[...] = dot(from_given[...], cotangent[...].reshape(288, 1024)).astype(BF16)
     key_row = lax.broadcasted_iota(jnp.int32, (1, 768), 1)
     key_row = lax.div(lax.rem(key_row, 48), 2) + lat * 12 - 6
     bias[...] = jnp.where((key_row >= 0) & (key_row < 96), near_bias[...], -jnp.inf)
@@ -211,14 +211,15 @@
 
     def side_copies(t):
         return (
-            copy_to(side_out.at[t, 0], side_in.at[t, 1], 4 + 4 * t, west),
-            copy_to(side_out.at[t, 1], side_in.at[t, 0], 5 + 4 * t, east),
+            copy_to(side_out.at[lax.rem(t, 2), 0], side_in.at[t, 1], 4 + 4 * t, west),
+            copy_to(side_out.at[lax.rem(t, 2), 1], side_in.at[t, 0], 5 + 4 * t, east),
         )
 
     def piece_copies(t):
+        out = piece_out.at[lax.rem(t, 2)]
         return (
-            copy_to(piece_out.at[t, part(0, 144)], piece_in.at[t, part(144, 144)], 6 + 4 * t, north),
-            copy_to(piece_out.at[t, part(144, 144)], piece_in.at[t, part(0, 144)], 7 + 4 * t, south),
+            copy_to(out.at[part(0, 144)], piece_in.at[t, part(144, 144)], 6 + 4 * t, north),
+            copy_to(out.at[part(144, 144)], piece_in.at[t, part(0, 144)], 7 + 4 * t, south),
         )
 
     def joined(out):
@@ -254,8 +255,8 @@
             acc[slot, keys, 0:256] += dot_tn(ds, qm)
             acc[slot, keys, 256:512] += dot_tn(pb, dm)
 
-        side_out[t, 0] = acc[slot, 0:288, :].astype(BF16)
-        side_out[t, 1] = acc[slot, 864:1152, :].astype(BF16)
+        side_out[slot, 0] = acc[slot, 0:288, :].astype(BF16)
+        side_out[slot, 1] = acc[slot, 864:1152, :].astype(BF16)
         for copy in side_copies(t):
             copy.start()
 
@@ -267,8 +268,8 @@
         high = mid.astype(BF16)
         low = (mid - high.astype(F32)).astype(BF16)
         parts = dot(from_middle[...], high)
-        piece_out[t, 0:144, :] = parts[0:144].astype(BF16)
-        piece_out[t, 144:288, :] = parts[432:576].astype(BF16)
+        piece_out[slot, 0:144, :] = parts[0:144].astype(BF16)
+        piece_out[slot, 144:288, :] = parts[432:576].astype(BF16)
         for copy in piece_copies(t):
             copy.start()
         own_kv[slot] = parts[144:432] + dot(from_middle[144:432, :], low)
@@ -276,9 +277,16 @@
     def pieces_back(t):
         for copy in piece_copies(t):
             copy.wait()
-        total = own_kv[lax.rem(t, 2)] + dot(from_piece[...], piece_in[t])
-        dqkv[:, tile(t, 1024)] = (total[:, 0:256] * 0.125).astype(BF16)
-        dqkv[:, tile(t, 2048)] = total[:, 256:512].astype(BF16)
+        both = own_kv[lax.rem(t, 2)] + dot(from_piece[...], piece_in[t])
+        dk, dv = (both[:, 0:256] * 0.125).astype(BF16), both[:, 256:512].astype(BF16)
+        dqkv[:, tile(t, 1024)] = dk
+        dqkv[:, tile(t, 2048)] = dv
+        for c in range(4):
+            rows = slice(256 * c, 256 * c + 256)
+            more = dot_nt(dk, w_qkv[rows, tile(t, 1024)]) + dot_nt(dv, w_qkv[rows, tile(t, 2048)])
+            total[:, rows] += more
+
+    total[...] = g[...].astype(F32)
 
     @pl.loop(0, 4)
     def _(t):
@@ -292,55 +300,59 @@
         def _():
             pieces_back(t - 2)
 
-    gots = (got_a, got_b)
+    mades, gots = (made_a, made_b), (got_a, got_b)
 
     def columns(job):
         return pl.ds(JOBS[job][1], JOBS[job][2])
 
-    def store_made(half, t, value):
-        made[half, t, :, :, :, :, 0:1024] = value.astype(BF16).reshape(2, 2, 4, 16, 1024)
-
     def make_a(half):
+        def store(t, value):
+            made_a[half, t] = value.astype(BF16).reshape(2, 2, 4, 16, 1024)
+
         @pl.when(half == 0)
         def _():
             @pl.loop(0, 4)
             def _(t):
-                store_made(half, t, dot_tn(xm[:, tile(t)], dqkv[:, 0:1024]))
+                store(t, dot_tn(xm[:, tile(t)], dqkv[:, 0:1024]))
 
         @pl.when(half == 1)
         def _():
             @pl.loop(0, 4)
             def _(t):
-                store_made(half, t, dot_tn(ctx[:, tile(t)], g[...]))
-
-    def make_b(half):
-        cols = pl.ds(pl.multiple_of(half * 1024 + 1024, 1024), 1024)
+                store(t, dot_tn(ctx[:, tile(t)], g[...]))
+
+    def make_b(n, half):
+        cols = pl.ds(pl.multiple_of(half * 1024 + 1024 + 256 * n, 256), 256)
 
         @pl.loop(0, 4)
         def _(t):
-            store_made(half, t, dot_tn(xm[:, tile(t)], dqkv[:, cols]))
+            value = dot_tn(xm[:, tile(t)], dqkv[:, cols]).astype(BF16)
+            made_b[half, t, :, :, :, :, 256 * n : 256 * n + 256] = value.reshape(2, 2, 4, 16, 256)
 
     def exchange(job):
         where = (EVERY,) * 5 + (columns(job),)
-        return copy_to(made.at[(1 - core, *where)], gots[JOBS[job][0]].at[where], 20 + job, partner)
+        phase = JOBS[job][0]
+        return copy_to(mades[phase].at[(1 - core, *where)], gots[phase].at[where], 20 + job, partner)
 
     def exchanged(job):
         exchange(job).wait()
-        cols, got = columns(job), gots[JOBS[job][0]]
+        cols, made, got = columns(job), mades[JOBS[job][0]], gots[JOBS[job][0]]
 
         @pl.loop(0, 4)
         def _(a):
             for b in range(2):
                 for c in range(2):
-                    total = made[core, a, b, c, :, :, cols].astype(F32)
-                    total = total + got[a, b, c, :, :, cols].astype(F32)
-                    made[core, a, b, c, :, :, cols] = total.astype(BF16)
+                    both = made[core, a, b, c, :, :, cols].astype(F32)
+                    both = both + got[a, b, c, :, :, cols].astype(F32)
+                    made[core, a, b, c, :, :, cols] = both.astype(BF16)
+
+        start(job, 0)
 
     def held(job, stage, at):
         order = JOBS[job][3]
         here = index_of(without(order, stage), order[stage], at)
         if stage == 0:
-            return made, (core, *here, EVERY, columns(job))
+            return mades[JOBS[job][0]], (core, *here, EVERY, columns(job))
         return scratch[job][2 * stage - 1], (*here, EVERY, EVERY)
 
     def stage_copies(job, stage):
@@ -349,7 +361,7 @@
         for by in (2, 1, 3):
             ref, where = held(job, stage, lax.rem(mine[axis] + by, 4))
             target = scratch[job][2 * stage].at[by - 1]
-            sem = 25 + job * 9 + stage * 3 + by - 1
+            sem = 20 + len(JOBS) + job * 9 + stage * 3 + by - 1
             copies.append(copy_to(ref.at[where], target, sem, device(axis, by)))
         return copies
 
@@ -366,6 +378,7 @@
             piece = piece + scratch[job][2 * stage][slot].astype(F32)
         if stage < 2:
             scratch[job][2 * stage + 1][...] = piece.astype(BF16)
+            start(job, stage + 1)
         else:
             final = (final_a, final_b)[JOBS[job][0]]
             final[:, columns(job)] = piece * (1.0 / 192.0)
@@ -373,65 +386,82 @@
     def swap(phase):
         rows = pl.ds(pl.multiple_of((1 - core) * 8, 8), 8)
         source = (final_a, final_b)[phase].at[rows, pl.ds(0, 1024)]
-        return copy_to(source, (cross_a, cross_b)[phase], 70 + phase, partner)
-
+        return copy_to(source, (cross_a, cross_b)[phase], 20 + 10 * len(JOBS) + phase, partner)
+
+    def group(n):
+        make_b(n, 1 - core)
+        for job in OF_QUAD[n]:
+            exchange(job).start()
+        make_b(n, core)
+
+    sides_back(3)
     make_a(1 - core)
     for job in (0, 1):
         exchange(job).start()
-    sides_back(3)
+    group(0)
     make_a(core)
     for job in (0, 1):
         exchanged(job)
-        start(job, 0)
-    pieces_back(2)
+    exchanged(2)
+    group(1)
+    exchanged(3)
 
     @pl.loop(0, 4)
     def _(t):
         cols = tile(t)
         value = xm[:, cols].astype(F32) + dot(ctx[...], w_out[:, cols])
-        value = dot(to_padded[...], value.astype(BF16)).astype(BF16)
-        block_out[:, :, :, cols] = value.reshape(2, 12, 16, 256)[:, :, 0:12, :]
-
-    for job in (0, 1):
+        value = dot(to_given[...], value.astype(BF16)).astype(BF16)
+        block_out[:, :, :, cols] = value.reshape(12, 12, 2, 256)
+        total[:, cols] += dot_nt(dqkv[:, 0:1024], w_qkv[cols, 0:1024])
+
+    pieces_back(2)
+    group(2)
+    for job in (0, 1, 2):
         reduced(job, 0)
-        start(job, 1)
+    for job in (4, 5):
+        exchanged(job)
+    reduced(3, 0)
     pieces_back(3)
-
-    make_b(1 - core)
-    for job in (2, 3):
-        exchange(job).start()
+    group(3)
+    for job in (6, 7):
+        exchanged(job)
 
     @pl.loop(0, 4)
     def _(t):
         cols = tile(t)
         hit = hits[...]
-        total = g[:, cols].astype(F32) + dot_nt(dqkv[...], w_qkv[cols, :])
-        kept = jnp.where(jnp.concatenate([hit, hit], axis=1) > 0.5, 0.0, total).astype(BF16)
-        kept = dot(to_padded[...], kept).astype(BF16)
-        grad_tokens[:, :, :, cols] = kept.reshape(2, 12, 16, 256)[:, :, 0:12, :]
-        high = total.astype(BF16)
-        low = (total - high.astype(F32)).astype(BF16)
+        value = total[:, cols]
+        high = value.astype(BF16)
+        low = (value - high.astype(F32)).astype(BF16)
         column = dot_tn(high, hit.astype(BF16)) + dot_tn(low, hit.astype(BF16))
         column = column.astype(BF16).reshape(2, 2, 4, 16, 128)
-        made[0, t, :, :, :, :, 1024:1152] = column
-        made[1, t, :, :, :, :, 1024:1152] = column
-
-    exchange(4).start()
-    make_b(core)
-    for job in (0, 1):
+        made_b[0, t, :, :, :, :, 1024:1152] = column
+        made_b[1, t, :, :, :, :, 1024:1152] = column
+
+    exchange(8).start()
+    for job in (0, 1, 2, 3):
         reduced(job, 1)
-        start(job, 2)
-    for job in (2, 3, 4):
-        exchanged(job)
-        start(job, 0)
+    exchanged(8)
+    for job in (4, 5):
+        reduced(job, 0)
+
+    @pl.loop(0, 4)
+    def _(t):
+        cols = tile(t)
+        hit = hits[...]
+        value = total[:, cols]
+        kept = jnp.where(jnp.concatenate([hit, hit], axis=1) > 0.5, 0.0, value).astype(BF16)
+        kept = dot(to_given[...], kept).astype(BF16)
+        grad_tokens[:, :, :, cols] = kept.reshape(12, 12, 2, 256)
+
+    for job in (6, 7, 8):
+        reduced(job, 0)
     for job in (0, 1):
         reduced(job, 2)
     swap(0).start()
-    for stage in (0, 1):
-        for job in (2, 3, 4):
-            reduced(job, stage)
-            start(job, stage + 1)
-    for job in (2, 3, 4):
+    for job in (4, 5, 6, 7, 8):
+        reduced(job, 1)
+    for job in (2, 3, 4, 5, 6, 7, 8):
         reduced(job, 2)
     swap(1).start()
     swap(0).wait()
@@ -454,10 +484,21 @@
         go[...] = final_a[rows, :]
 
 
+def hand_out_kernel(block_out, grad_tokens, gq, go, gm, *targets):
+    for source, target in zip((block_out, grad_tokens, gq, go), targets):
+        target[...] = source[...]
+    row = lax.broadcasted_iota(jnp.int32, (8, 128), 0)
+    lane = lax.broadcasted_iota(jnp.int32, (8, 128), 1)
+    targets[4][...] = jnp.sum(jnp.where(row == lane, gm[...], 0.0), axis=0)[0:8]
+
+
 def local(tokens, masked, mask_embed, w_qkv, w_out, cotangent):
-    natural = one_hot(padded_order(), 384)
+    given = one_hot(given_order(), 288)
     piece, middle = one_hot(piece_order(), 288), one_hot(middle_order(), 576)
-    orders = [natural, natural.T, piece, piece.T, middle, middle.T]
+    orders = [given, given.T, piece, piece.T, middle, middle.T]
+    row, lev = np.arange(288) % 24 // 2, np.arange(288) % 2
+    place = lev * 144 + row * 12 + np.arange(288) // 24
+    place = np.broadcast_to(place[:, None], (288, 144)).astype(np.int32)
     near_bias = np.where(near(), 0.0, -np.inf).astype(np.float32)
     vmem, hbm = pl.BlockSpec(memory_space=pltpu.VMEM), pl.BlockSpec(memory_space=pl.ANY)
     jobs = []
@@ -470,18 +511,17 @@
     block_out, grad_tokens, gq, go, gm = pl.pallas_call(
         block_kernel,
         out_shape=(
-            jax.ShapeDtypeStruct(tokens.shape, BF16),
-            jax.ShapeDtypeStruct(tokens.shape, BF16),
+            jax.ShapeDtypeStruct((12, 12, 2, 1024), BF16),
+            jax.ShapeDtypeStruct((12, 12, 2, 1024), BF16),
             jax.ShapeDtypeStruct((8, 3072), F32),
             jax.ShapeDtypeStruct((8, 1024), F32),
             jax.ShapeDtypeStruct((8, 128), F32),
         ),
-        in_specs=[vmem, vmem, vmem, hbm, hbm, vmem, vmem] + [vmem] * 6,
+        in_specs=[vmem, vmem, vmem, vmem, hbm, hbm, vmem, vmem] + [vmem] * 6,
         out_specs=(vmem,) * 5,
         scratch_shapes=[
             pltpu.VMEM((1024, 3072), BF16),
             pltpu.VMEM((1024, 1024), BF16),
-            pltpu.VMEM((24, 16, 1024), BF16),
             pltpu.VMEM((288, 1024), BF16),
             pltpu.VMEM((288, 1024), BF16),
             pltpu.VMEM((96, 768), F32),
@@ -495,11 +535,13 @@
             pltpu.VMEM((288, 1024), BF16),
             pltpu.VMEM((1152, 2048), BF16),
             pltpu.VMEM((2, 1152, 512), F32),
+            pltpu.VMEM((2, 2, 288, 512), BF16),
             pltpu.VMEM((4, 2, 288, 512), BF16),
-            pltpu.VMEM((4, 2, 288, 512), BF16),
-            pltpu.VMEM((4, 288, 512), BF16),
+            pltpu.VMEM((2, 288, 512), BF16),
             pltpu.VMEM((4, 288, 512), BF16),
             pltpu.VMEM((2, 288, 512), F32),
+            pltpu.VMEM((288, 1024), F32),
+            pltpu.VMEM((2, 4, 2, 2, 4, 16, 1024), BF16),
             pltpu.VMEM((2, 4, 2, 2, 4, 16, 1152), BF16),
             pltpu.VMEM((4, 2, 2, 4, 16, 1024), BF16),
             pltpu.VMEM((4, 2, 2, 4, 16, 1152), BF16),
@@ -509,18 +551,33 @@
             pltpu.VMEM((8, 1024), F32),
             pltpu.VMEM((8, 1024), F32),
             pltpu.SemaphoreType.DMA((2,)),
-            pltpu.SemaphoreType.DMA((72,)),
-            pltpu.SemaphoreType.DMA((72,)),
+            pltpu.SemaphoreType.DMA((22 + 10 * len(JOBS),)),
+            pltpu.SemaphoreType.DMA((22 + 10 * len(JOBS),)),
         ],
         compiler_params=pltpu.CompilerParams(
             collective_id=1, has_side_effects=True, vmem_limit_bytes=62 * 1024 * 1024
         ),
         name="attention_block",
     )(
-        tokens, masked, mask_embed[None], w_qkv, w_out, cotangent, jnp.asarray(near_bias),
+        tokens.transpose(1, 2, 0, 3), masked, jnp.asarray(place), mask_embed.reshape(8, 128), w_qkv, w_out,
+        cotangent.transpose(1, 2, 0, 3), jnp.asarray(near_bias),
         *[jnp.asarray(order, BF16) for order in orders],
     )
-    return (block_out, grad_tokens, gq, go, gm[:, 0])
+    block_out, grad_tokens, gq, go, gm = pl.pallas_call(
+        hand_out_kernel,
+        out_shape=(
+            jax.ShapeDtypeStruct((12, 12, 2, 1024), BF16),
+            jax.ShapeDtypeStruct((12, 12, 2, 1024), BF16),
+            jax.ShapeDtypeStruct((8, 3072), F32),
+            jax.ShapeDtypeStruct((8, 1024), F32),
+            jax.ShapeDtypeStruct((8,), F32),
+        ),
+        in_specs=[vmem] * 5,
+        out_specs=(vmem,) * 5,
+        name="hand_out",
+    )(block_out, grad_tokens, gq, go, gm)
+    block_out, grad_tokens = block_out.transpose(2, 0, 1, 3), grad_tokens.transpose(2, 0, 1, 3)
+    return (block_out, grad_tokens, gq, go, gm)
 
 
 def solution(mesh):

time: 147 us -> 137 us (0.932)
  local copies, waits for them, and re-layouts: 14.8 us -> 0 us
  Pallas kernels: 131 us -> 136 us
    unnamed x6 -> x0, local copies, waits for them, and re-layouts: 12.3 us -> none
    pallas_call x1 -> x2, Pallas kernels: 131 us -> 136 us  [the longest x1 134 us: local(): pl.pallas_call(block_kernel, out_shape=(jax.ShapeDtypeStruct((12, 12, 2,...]
where the time goes in v2:
time: 137 us
  Pallas kernels  136 us (99%)
    pallas_call x1, Pallas kernels, local(): pl.pallas_call(block_kernel, out_shape=(jax.ShapeDtypeStruct((12, 12, 2,...  134 us

profile of v2, /device:TPU:1, one launch (start us, length us, event | category | flops | bytes accessed | tf_op | source)
XLA Modules:
  0.0 137.0 jit_solution(17123242882691282178)
XLA Ops:
  0.6 134.0 %attention_block.1 = (bf16[12,12,2,1024]{3,2,1,0:T(2,128)(2,1)}, bf16[12,12,2,1024]{3,2,1,0:T(2,128)(2,1)}, f32[8,3072]{1,0:T(8,128)}, f32[8,1024]{1,0:T(8,128)}, f32[8,128]{1,0:T(8,128)}) custom-call(bf16[12,12,2,1024]{3,2,1,0:T(2,128)(2,1)} %bitcast.5, s32[1,1,144]{2,1,0:T(1,128)} %masked.1, s32[288,144]{1,0:T(8,128)} %constant.14.clone.place, ...), custom_call_target="tpu_custom_call" | custom-call | tf_op jit(solution)/shard_map/attention_block/pallas_call | solution.py:511
  134.6 2.3 %hand_out.1 = (bf16[12,12,2,1024]{3,2,1,0:T(2,128)(2,1)}, bf16[12,12,2,1024]{3,2,1,0:T(2,128)(2,1)}, f32[8,3072]{1,0:T(8,128)}, f32[8,1024]{1,0:T(8,128)}, f32[8]{0:T(128)}) custom-call(bf16[12,12,2,1024]{3,2,1,0:T(2,128)(2,1)} %get-tuple-element.15.block_out, bf16[12,12,2,1024]{3,2,1,0:T(2,128)(2,1)} %get-tuple-element.16.grad_tokens, ...), custom_call_target="tpu_custom_call" | custom-call | tf_op jit(solution)/shard_map/hand_out/pallas_call | solution.py:566

commit v3 on v2

--- a/solution.py
+++ b/solution.py
@@ -16,17 +16,17 @@
 
 
 JOBS = (
-    (0, 0, 512, "zyx"),
-    (0, 512, 512, "yzx"),
-    (1, 0, 256, "zyx"),
-    (1, 256, 256, "yzx"),
-    (1, 512, 128, "zyx"),
-    (1, 640, 128, "yzx"),
+    (0, 0, 384, "zyx"),
+    (0, 384, 384, "yxz"),
+    (0, 768, 256, "xzy"),
+    (1, 0, 256, "xzy"),
+    (1, 256, 256, "zyx"),
+    (1, 512, 256, "yxz"),
     (1, 768, 128, "xzy"),
     (1, 896, 128, "yxz"),
     (1, 1024, 128, "zyx"),
 )
-OF_QUAD = ((2,), (3,), (4, 5), (6, 7))
+OF_QUAD = ((3,), (4,), (5,), (6, 7))
 
 
 def piece_order():
@@ -52,13 +52,12 @@
     return (order[:, None] == np.arange(size)[None, :]).astype(np.float32)
 
 
-def near():
-    query = np.arange(96)
-    key = np.arange(768)
-    row, column = query % 24 // 2, query // 24
-    krow, kcolumn = key % 48 // 2, key // 48
-    allowed = (krow[None] >= row[:, None]) & (krow[None] <= row[:, None] + 11)
-    return allowed & (kcolumn[None] >= column[:, None]) & (kcolumn[None] <= column[:, None] + 11)
+def near(shift):
+    inner, outer = np.arange(96), np.arange(768)
+    row = outer[None] % 48 // 2 - inner[:, None] % 24 // 2 - shift
+    column = outer[None] // 48 - inner[:, None] // 24 - shift
+    allowed = (row >= 0) & (row <= 11) & (column >= 0) & (column <= 11)
+    return np.where(allowed, 0.0, -np.inf).astype(np.float32)
 
 
 def dot(a, b):
@@ -92,11 +91,12 @@
 
 
 def block_kernel(
-    tokens, masked, place, embed, w_qkv_hbm, w_out_hbm, cotangent, near_bias,
-    from_given, to_given, to_piece, from_piece, to_middle, from_middle,
+    tokens, masked, place, embed, w_qkv_hbm, w_out_hbm, cotangent_hbm, near_keys_hbm, near_queries_hbm,
+    from_given, to_given, to_piece, to_middle_hbm,
     block_out, grad_tokens, gq, go, gm,
-    w_qkv, w_out, xm, g, bias, hits, ctx, dqkv,
-    pieces, stacked, ext, q, d, kv, acc, side_out, side_in, piece_out, piece_in, own_kv,
+    w_qkv, w_out, cotangent, near_keys, near_queries, to_middle, xm, g, key_bias, query_bias, hits, ctx, dqkv,
+    pieces, stacked, ext, g_pieces, g_stacked, g_ext,
+    stats, stat_pieces, stat_stacked, stat_ext, stat_rows, q, d, kv, own_kv, ext_q, ext_d,
     total, made_a, made_b, got_a, got_b, *rest,
 ):
     scratch = [rest[5 * i : 5 * i + 5] for i in range(len(JOBS))]
@@ -127,10 +127,15 @@
     for other in greeted:
         pl.semaphore_signal(barrier, inc=1, device_id=other, device_id_type=MESH)
 
-    loads = (
-        pltpu.make_async_copy(w_qkv_hbm, w_qkv, load.at[0]),
-        pltpu.make_async_copy(w_out_hbm, w_out, load.at[1]),
+    loaded = (
+        (cotangent_hbm, cotangent),
+        (near_keys_hbm, near_keys),
+        (near_queries_hbm, near_queries),
+        (to_middle_hbm, to_middle),
+        (w_qkv_hbm, w_qkv),
+        (w_out_hbm, w_out),
     )
+    loads = [pltpu.make_async_copy(*pair, load.at[i]) for i, pair in enumerate(loaded)]
     for copy in loads:
         copy.start()
 
@@ -161,35 +166,65 @@
     def tile(t, start=0):
         return pl.ds(pl.multiple_of(t * 256 + start, 256), 256)
 
-    first = (
-        copy_to(pieces.at[part(0, 144)], stacked.at[part(432, 144)], 0, north),
-        copy_to(pieces.at[part(144, 144)], stacked.at[part(0, 144)], 1, south),
-    )
-    for copy in first:
-        copy.start()
-
+    def to_neighbours(source, target, sem):
+        return (
+            copy_to(source.at[part(0, 144)], target.at[part(432, 144)], sem, north),
+            copy_to(source.at[part(144, 144)], target.at[part(0, 144)], sem + 1, south),
+        )
+
+    def to_sides(whole, sem):
+        return (
+            copy_to(whole.at[part(288, 288)], whole.at[part(864, 288)], sem, west),
+            copy_to(whole.at[part(576, 288)], whole.at[part(0, 288)], sem + 1, east),
+        )
+
+    def begin(copies):
+        for copy in copies:
+            copy.start()
+
+    def finish(copies):
+        for copy in copies:
+            copy.wait()
+
+    def reordered(matrix, value):
+        high = value.astype(BF16)
+        rest_of = value - high.astype(F32)
+        middle = rest_of.astype(BF16)
+        low = (rest_of - middle.astype(F32)).astype(BF16)
+        return (dot(matrix, high) + dot(matrix, middle)) + dot(matrix, low)
+
+    rows_moved = to_neighbours(pieces, stacked, 0)
+    sides_moved = to_sides(ext, 2)
+    g_rows_moved = to_neighbours(g_pieces, g_stacked, 4)
+    g_sides_moved = to_sides(g_ext, 6)
+    stat_rows_moved = to_neighbours(stat_pieces, stat_stacked, 8)
+    stat_sides_moved = to_sides(stat_ext, 10)
+    begin(rows_moved)
+
+    finish(loads[:4])
     g[...] = dot(from_given[...], cotangent[...].reshape(288, 1024)).astype(BF16)
-    key_row = lax.broadcasted_iota(jnp.int32, (1, 768), 1)
-    key_row = lax.div(lax.rem(key_row, 48), 2) + lat * 12 - 6
-    bias[...] = jnp.where((key_row >= 0) & (key_row < 96), near_bias[...], -jnp.inf)
-    for copy in loads:
-        copy.wait()
+    g_pieces[...] = dot(to_piece[...], g[...]).astype(BF16)
+    g_stacked[144:432, :] = g[...]
+    total[...] = g[...].astype(F32)
+    stats[...] = jnp.zeros((288, 128), F32)
+    ext_row = lax.broadcasted_iota(jnp.int32, (1, 768), 1)
+    ext_row = lax.div(lax.rem(ext_row, 48), 2) + lat * 12 - 6
+    on_grid = (ext_row >= 0) & (ext_row < 96)
+    key_bias[...] = jnp.where(on_grid, near_keys[...], -jnp.inf)
+    query_bias[...] = jnp.where(on_grid, near_queries[...], -jnp.inf)
+    finish(loads[4:])
 
     @pl.loop(0, 4)
     def _(t):
         cols = tile(t)
         q[:, cols] = dot(xm[...], w_qkv[:, cols]).astype(BF16)
         d[:, cols] = dot_nt(g[...], w_out[cols, :]).astype(BF16)
-
-    for copy in first:
-        copy.wait()
+        own_kv[:, cols] = dot(xm[...], w_qkv[:, tile(t, 1024)]).astype(BF16)
+        own_kv[:, tile(t, 1024)] = dot(xm[...], w_qkv[:, tile(t, 2048)]).astype(BF16)
+
+    finish(rows_moved)
     ext[288:864, :] = dot(to_middle[...], stacked[...]).astype(BF16)
-    second = (
-        copy_to(ext.at[part(288, 288)], ext.at[part(864, 288)], 2, west),
-        copy_to(ext.at[part(576, 288)], ext.at[part(0, 288)], 3, east),
-    )
-    for copy in second:
-        copy.start()
+    begin(sides_moved)
 
     def project(start, rows):
         @pl.loop(0, 8)
@@ -198,107 +233,100 @@
                 ext[start : start + rows, :], w_qkv[:, tile(t, 1024)]
             ).astype(BF16)
 
+    def project_queries(start, rows):
+        @pl.loop(0, 4)
+        def _(t):
+            ext_q[start : start + rows, tile(t)] = dot(
+                ext[start : start + rows, :], w_qkv[:, tile(t)]
+            ).astype(BF16)
+
     project(288, 576)
-    for copy in second:
-        copy.wait()
+    project_queries(288, 576)
+    finish(sides_moved)
+    begin(g_rows_moved)
     project(0, 288)
     project(864, 288)
 
     lane_head = lax.div(lax.broadcasted_iota(jnp.int32, (96, 256), 1), 64)
     picks = [lane_head == h for h in range(4)]
     nothing = jnp.zeros((96, 256), BF16)
+    stat_lane = lax.broadcasted_iota(jnp.int32, (96, 128), 1)
     factor = math.log2(math.e) / 8.0
 
-    def side_copies(t):
-        return (
-            copy_to(side_out.at[lax.rem(t, 2), 0], side_in.at[t, 1], 4 + 4 * t, west),
-            copy_to(side_out.at[lax.rem(t, 2), 1], side_in.at[t, 0], 5 + 4 * t, east),
-        )
-
-    def piece_copies(t):
-        out = piece_out.at[lax.rem(t, 2)]
-        return (
-            copy_to(out.at[part(0, 144)], piece_in.at[t, part(144, 144)], 6 + 4 * t, north),
-            copy_to(out.at[part(144, 144)], piece_in.at[t, part(0, 144)], 7 + 4 * t, south),
-        )
+    def apart(block):
+        return jnp.concatenate([jnp.where(pick, block, nothing) for pick in picks], axis=0)
 
     def joined(out):
-        total = jnp.where(picks[0], out[0:96], 0.0)
+        whole = jnp.where(picks[0], out[0:96], 0.0)
         for h in range(1, 4):
-            total = jnp.where(picks[h], out[h * 96 : h * 96 + 96], total)
-        return total
-
-    def quad(t):
+            whole = jnp.where(picks[h], out[h * 96 : h * 96 + 96], whole)
+        return whole
+
+    def queries(t):
         cols, vcols = tile(t), tile(t, 1024)
-        slot = lax.rem(t, 2)
-        acc[slot] = jnp.zeros((1152, 512), F32)
 
         @pl.loop(0, 3)
         def _(j):
             rows = pl.ds(pl.multiple_of(j * 96, 96), 96)
             keys = pl.ds(pl.multiple_of(j * 192, 192), 768)
-            qj, dj = q[rows, cols], d[rows, cols]
-            qm = jnp.concatenate([jnp.where(pick, qj, nothing) for pick in picks], axis=0)
-            dm = jnp.concatenate([jnp.where(pick, dj, nothing) for pick in picks], axis=0)
+            qm, dm = apart(q[rows, cols]), apart(d[rows, cols])
             kw, vw = kv[keys, cols], kv[keys, vcols]
-            s = dot_nt(qm, kw).reshape(4, 96, 768) + bias[...][None]
+            s = dot_nt(qm, kw).reshape(4, 96, 768) + key_bias[...][None]
             top = jnp.max(s, axis=-1, keepdims=True)
             e = jnp.exp2((s - top) * factor)
-            p = e * (1.0 / jnp.sum(e, axis=-1, keepdims=True))
-            p = p.reshape(384, 768)
-            pb = p.astype(BF16)
-            out = dot(pb, vw)
+            share = 1.0 / jnp.sum(e, axis=-1, keepdims=True)
+            p = (e * share).reshape(384, 768)
+            out = dot(p.astype(BF16), vw)
             delta = jnp.sum(out * dm.astype(F32), axis=-1, keepdims=True)
             ctx[rows, cols] = joined(out).astype(BF16)
             ds = (p * (dot_nt(dm, vw) - delta)).astype(BF16)
             dqkv[rows, cols] = (joined(dot(ds, kw)) * 0.125).astype(BF16)
-            acc[slot, keys, 0:256] += dot_tn(ds, qm)
-            acc[slot, keys, 256:512] += dot_tn(pb, dm)
-
-        side_out[slot, 0] = acc[slot, 0:288, :].astype(BF16)
-        side_out[slot, 1] = acc[slot, 864:1152, :].astype(BF16)
-        for copy in side_copies(t):
-            copy.start()
-
-    def sides_back(t):
-        for copy in side_copies(t):
-            copy.wait()
-        slot = lax.rem(t, 2)
-        mid = acc[slot, 288:864, :] + side_in[t].astype(F32).reshape(576, 512)
-        high = mid.astype(BF16)
-        low = (mid - high.astype(F32)).astype(BF16)
-        parts = dot(from_middle[...], high)
-        piece_out[slot, 0:144, :] = parts[0:144].astype(BF16)
-        piece_out[slot, 144:288, :] = parts[432:576].astype(BF16)
-        for copy in piece_copies(t):
-            copy.start()
-        own_kv[slot] = parts[144:432] + dot(from_middle[144:432, :], low)
-
-    def pieces_back(t):
-        for copy in piece_copies(t):
-            copy.wait()
-        both = own_kv[lax.rem(t, 2)] + dot(from_piece[...], piece_in[t])
-        dk, dv = (both[:, 0:256] * 0.125).astype(BF16), both[:, 256:512].astype(BF16)
-        dqkv[:, tile(t, 1024)] = dk
-        dqkv[:, tile(t, 2048)] = dv
+            kept = stats[rows, :]
+            for h in range(4):
+                values = (top[h], share[h], delta[h * 96 : h * 96 + 96])
+                for kind, value in enumerate(values):
+                    kept = jnp.where(stat_lane == t * 16 + kind * 4 + h, value, kept)
+            stats[rows, :] = kept
+
+    def keys_of(t):
+        cols, vcols = tile(t), tile(t, 1024)
+
+        @pl.loop(0, 3)
+        def _(j):
+            rows = pl.ds(pl.multiple_of(j * 96, 96), 96)
+            seen = pl.ds(pl.multiple_of(j * 192, 192), 768)
+            km, vm = apart(own_kv[rows, cols]), apart(own_kv[rows, vcols])
+            qw, dw = ext_q[seen, cols], ext_d[seen, cols]
+            known = stat_rows[j, 16 * t : 16 * t + 16, :]
+            top, share, delta = (known[4 * i : 4 * i + 4].reshape(4, 1, 768) for i in range(3))
+            s = dot_nt(km, qw).reshape(4, 96, 768) + query_bias[...][None]
+            p = jnp.exp2((s - top) * factor) * share
+            ds = p * (dot_nt(vm, dw).reshape(4, 96, 768) - delta)
+            dk = joined(dot(ds.reshape(384, 768).astype(BF16), qw)) * 0.125
+            dv = joined(dot(p.reshape(384, 768).astype(BF16), dw))
+            dqkv[rows, tile(t, 1024)] = dk.astype(BF16)
+            dqkv[rows, tile(t, 2048)] = dv.astype(BF16)
+
+    def add_to_total(t):
+        dk, dv = dqkv[:, tile(t, 1024)], dqkv[:, tile(t, 2048)]
         for c in range(4):
             rows = slice(256 * c, 256 * c + 256)
             more = dot_nt(dk, w_qkv[rows, tile(t, 1024)]) + dot_nt(dv, w_qkv[rows, tile(t, 2048)])
             total[:, rows] += more
 
-    total[...] = g[...].astype(F32)
-
     @pl.loop(0, 4)
     def _(t):
-        quad(t)
-
-        @pl.when(t >= 1)
+        queries(t)
+
+        @pl.when(t == 2)
         def _():
-            sides_back(t - 1)
-
-        @pl.when(t >= 2)
-        def _():
-            pieces_back(t - 2)
+            finish(g_rows_moved)
+            g_ext[288:864, :] = dot(to_middle[...], g_stacked[...]).astype(BF16)
+            begin(g_sides_moved)
+
+    stat_pieces[...] = reordered(to_piece[...], stats[...])
+    stat_stacked[144:432, :] = stats[...]
+    begin(stat_rows_moved)
 
     mades, gots = (made_a, made_b), (got_a, got_b)
 
@@ -332,7 +360,7 @@
     def exchange(job):
         where = (EVERY,) * 5 + (columns(job),)
         phase = JOBS[job][0]
-        return copy_to(mades[phase].at[(1 - core, *where)], gots[phase].at[where], 20 + job, partner)
+        return copy_to(mades[phase].at[(1 - core, *where)], gots[phase].at[where], 12 + job, partner)
 
     def exchanged(job):
         exchange(job).wait()
@@ -361,7 +389,7 @@
         for by in (2, 1, 3):
             ref, where = held(job, stage, lax.rem(mine[axis] + by, 4))
             target = scratch[job][2 * stage].at[by - 1]
-            sem = 20 + len(JOBS) + job * 9 + stage * 3 + by - 1
+            sem = 12 + len(JOBS) + job * 9 + stage * 3 + by - 1
             copies.append(copy_to(ref.at[where], target, sem, device(axis, by)))
         return copies
 
@@ -386,7 +414,7 @@
     def swap(phase):
         rows = pl.ds(pl.multiple_of((1 - core) * 8, 8), 8)
         source = (final_a, final_b)[phase].at[rows, pl.ds(0, 1024)]
-        return copy_to(source, (cross_a, cross_b)[phase], 20 + 10 * len(JOBS) + phase, partner)
+        return copy_to(source, (cross_a, cross_b)[phase], 12 + 10 * len(JOBS) + phase, partner)
 
     def group(n):
         make_b(n, 1 - core)
@@ -394,17 +422,44 @@
             exchange(job).start()
         make_b(n, core)
 
-    sides_back(3)
     make_a(1 - core)
-    for job in (0, 1):
+    for job in (0, 1, 2):
         exchange(job).start()
+
+    project_queries(0, 288)
+    project_queries(864, 288)
+    finish(stat_rows_moved)
+    stat_ext[288:864, :] = reordered(to_middle[...], stat_stacked[...])
+    finish(g_sides_moved)
+    begin(stat_sides_moved)
+    make_a(core)
+    for job in (0, 1, 2):
+        exchanged(job)
+
+    @pl.loop(0, 4)
+    def _(t):
+        ext_d[:, tile(t)] = dot_nt(g_ext[...], w_out[tile(t), :]).astype(BF16)
+
+    finish(stat_sides_moved)
+    for j in range(3):
+        stat_rows[j] = stat_ext[192 * j : 192 * j + 768, :].T
+
+    def advance(*steps):
+        for job, stage in steps:
+            reduced(job, stage)
+
+    keys_of(0)
     group(0)
-    make_a(core)
-    for job in (0, 1):
-        exchanged(job)
-    exchanged(2)
+    add_to_total(0)
+    exchanged(3)
+    keys_of(1)
+    advance((0, 0), (1, 0), (2, 0))
     group(1)
-    exchanged(3)
+    add_to_total(1)
+    exchanged(4)
+    keys_of(2)
+    advance((0, 1), (1, 1), (2, 1), (3, 0))
+    group(2)
 
     @pl.loop(0, 4)
     def _(t):
@@ -414,17 +469,14 @@
         block_out[:, :, :, cols] = value.reshape(12, 12, 2, 256)
         total[:, cols] += dot_nt(dqkv[:, 0:1024], w_qkv[cols, 0:1024])
 
-    pieces_back(2)
-    group(2)
-    for job in (0, 1, 2):
-        reduced(job, 0)
-    for job in (4, 5):
-        exchanged(job)
-    reduced(3, 0)
-    pieces_back(3)
+    add_to_total(2)
+    exchanged(5)
+    keys_of(3)
     group(3)
-    for job in (6, 7):
-        exchanged(job)
+    advance((3, 1), (4, 0))
+    add_to_total(3)
+    exchanged(6)
+    exchanged(7)
 
     @pl.loop(0, 4)
     def _(t):
@@ -439,11 +491,10 @@
         made_b[1, t, :, :, :, :, 1024:1152] = column
 
     exchange(8).start()
-    for job in (0, 1, 2, 3):
-        reduced(job, 1)
+    advance((0, 2), (1, 2), (2, 2))
+    swap(0).start()
+    advance((4, 1), (5, 0))
     exchanged(8)
-    for job in (4, 5):
-        reduced(job, 0)
 
     @pl.loop(0, 4)
     def _(t):
@@ -454,15 +505,8 @@
         kept = dot(to_given[...], kept).astype(BF16)
         grad_tokens[:, :, :, cols] = kept.reshape(12, 12, 2, 256)
 
-    for job in (6, 7, 8):
-        reduced(job, 0)
-    for job in (0, 1):
-        reduced(job, 2)
-    swap(0).start()
-    for job in (4, 5, 6, 7, 8):
-        reduced(job, 1)
-    for job in (2, 3, 4, 5, 6, 7, 8):
-        reduced(job, 2)
+    advance((3, 2), (6, 0), (7, 0), (5, 1), (8, 0), (4, 2), (6, 1), (7, 1), (8, 1))
+    advance((5, 2), (6, 2), (7, 2), (8, 2))
     swap(1).start()
     swap(0).wait()
     swap(1).wait()
@@ -495,11 +539,10 @@
 def local(tokens, masked, mask_embed, w_qkv, w_out, cotangent):
     given = one_hot(given_order(), 288)
     piece, middle = one_hot(piece_order(), 288), one_hot(middle_order(), 576)
-    orders = [given, given.T, piece, piece.T, middle, middle.T]
+    orders = [given, given.T, piece, middle]
     row, lev = np.arange(288) % 24 // 2, np.arange(288) % 2
     place = lev * 144 + row * 12 + np.arange(288) // 24
     place = np.broadcast_to(place[:, None], (288, 144)).astype(np.int32)
-    near_bias = np.where(near(), 0.0, -np.inf).astype(np.float32)
     vmem, hbm = pl.BlockSpec(memory_space=pltpu.VMEM), pl.BlockSpec(memory_space=pl.ANY)
     jobs = []
     for _, _, wide, order in JOBS:
@@ -517,13 +560,18 @@
             jax.ShapeDtypeStruct((8, 1024), F32),
             jax.ShapeDtypeStruct((8, 128), F32),
         ),
-        in_specs=[vmem, vmem, vmem, vmem, hbm, hbm, vmem, vmem] + [vmem] * 6,
+        in_specs=[vmem] * 4 + [hbm] * 5 + [vmem] * 3 + [hbm],
         out_specs=(vmem,) * 5,
         scratch_shapes=[
             pltpu.VMEM((1024, 3072), BF16),
             pltpu.VMEM((1024, 1024), BF16),
+            pltpu.VMEM((12, 12, 2, 1024), BF16),
+            pltpu.VMEM((96, 768), F32),
+            pltpu.VMEM((96, 768), F32),
+            pltpu.VMEM((576, 576), BF16),
             pltpu.VMEM((288, 1024), BF16),
             pltpu.VMEM((288, 1024), BF16),
+            pltpu.VMEM((96, 768), F32),
             pltpu.VMEM((96, 768), F32),
             pltpu.VMEM((288, 128), F32),
             pltpu.VMEM((288, 1024), BF16),
@@ -532,14 +580,19 @@
             pltpu.VMEM((576, 1024), BF16),
             pltpu.VMEM((1152, 1024), BF16),
             pltpu.VMEM((288, 1024), BF16),
+            pltpu.VMEM((576, 1024), BF16),
+            pltpu.VMEM((1152, 1024), BF16),
+            pltpu.VMEM((288, 128), F32),
+            pltpu.VMEM((288, 128), F32),
+            pltpu.VMEM((576, 128), F32),
+            pltpu.VMEM((1152, 128), F32),
+            pltpu.VMEM((3, 128, 768), F32),
+            pltpu.VMEM((288, 1024), BF16),
             pltpu.VMEM((288, 1024), BF16),
             pltpu.VMEM((1152, 2048), BF16),
-            pltpu.VMEM((2, 1152, 512), F32),
-            pltpu.VMEM((2, 2, 288, 512), BF16),
-            pltpu.VMEM((4, 2, 288, 512), BF16),
-            pltpu.VMEM((2, 288, 512), BF16),
-            pltpu.VMEM((4, 288, 512), BF16),
-            pltpu.VMEM((2, 288, 512), F32),
+            pltpu.VMEM((288, 2048), BF16),
+            pltpu.VMEM((1152, 1024), BF16),
+            pltpu.VMEM((1152, 1024), BF16),
             pltpu.VMEM((288, 1024), F32),
             pltpu.VMEM((2, 4, 2, 2, 4, 16, 1024), BF16),
             pltpu.VMEM((2, 4, 2, 2, 4, 16, 1152), BF16),
@@ -550,9 +603,9 @@
             pltpu.VMEM((16, 1152), F32),
             pltpu.VMEM((8, 1024), F32),
             pltpu.VMEM((8, 1024), F32),
-            pltpu.SemaphoreType.DMA((2,)),
-            pltpu.SemaphoreType.DMA((22 + 10 * len(JOBS),)),
-            pltpu.SemaphoreType.DMA((22 + 10 * len(JOBS),)),
+            pltpu.SemaphoreType.DMA((6,)),
+            pltpu.SemaphoreType.DMA((14 + 10 * len(JOBS),)),
+            pltpu.SemaphoreType.DMA((14 + 10 * len(JOBS),)),
         ],
         compiler_params=pltpu.CompilerParams(
             collective_id=1, has_side_effects=True, vmem_limit_bytes=62 * 1024 * 1024
@@ -560,7 +613,7 @@
         name="attention_block",
     )(
         tokens.transpose(1, 2, 0, 3), masked, jnp.asarray(place), mask_embed.reshape(8, 128), w_qkv, w_out,
-        cotangent.transpose(1, 2, 0, 3), jnp.asarray(near_bias),
+        cotangent.transpose(1, 2, 0, 3), jnp.asarray(near(0)), jnp.asarray(near(1)),
         *[jnp.asarray(order, BF16) for order in orders],
     )
     block_out, grad_tokens, gq, go, gm = pl.pallas_call(

time: 137 us -> 127 us (0.927)
  Pallas kernels: 136 us -> 126 us
    pallas_call x1, Pallas kernels: 134 us -> 124 us  [local(): pl.pallas_call(block_kernel, out_shape=(jax.ShapeDtypeStruct((12, 12, 2,...]
where the time goes in v3:
time: 127 us
  Pallas kernels  126 us (99%)
    pallas_call x1, Pallas kernels, local(): pl.pallas_call(block_kernel, out_shape=(jax.ShapeDtypeStruct((12, 12, 2,...  124 us

profile of v3, /device:TPU:1, one launch (start us, length us, event | category | flops | bytes accessed | tf_op | source)
XLA Modules:
  0.0 126.9 jit_solution(17256184902354166248)
XLA Ops:
  0.6 123.9 %attention_block.1 = (bf16[12,12,2,1024]{3,2,1,0:T(2,128)(2,1)}, bf16[12,12,2,1024]{3,2,1,0:T(2,128)(2,1)}, f32[8,3072]{1,0:T(8,128)}, f32[8,1024]{1,0:T(8,128)}, f32[8,128]{1,0:T(8,128)}) custom-call(bf16[12,12,2,1024]{3,2,1,0:T(2,128)(2,1)} %bitcast.5, s32[1,1,144]{2,1,0:T(1,128)} %masked.1, s32[288,144]{1,0:T(8,128)} %constant.12.clone.place, ...), custom_call_target="tpu_custom_call" | custom-call | tf_op jit(solution)/shard_map/attention_block/pallas_call | solution.py:554
  124.5 2.3 %hand_out.1 = (bf16[12,12,2,1024]{3,2,1,0:T(2,128)(2,1)}, bf16[12,12,2,1024]{3,2,1,0:T(2,128)(2,1)}, f32[8,3072]{1,0:T(8,128)}, f32[8,1024]{1,0:T(8,128)}, f32[8]{0:T(128)}) custom-call(bf16[12,12,2,1024]{3,2,1,0:T(2,128)(2,1)} %get-tuple-element.15.block_out, bf16[12,12,2,1024]{3,2,1,0:T(2,128)(2,1)} %get-tuple-element.16.grad_tokens, ...), custom_call_target="tpu_custom_call" | custom-call | tf_op jit(solution)/shard_map/hand_out/pallas_call | solution.py:619

commit v4 on v3

--- a/solution.py
+++ b/solution.py
@@ -91,13 +91,13 @@
 
 
 def block_kernel(
-    tokens, masked, place, embed, w_qkv_hbm, w_out_hbm, cotangent_hbm, near_keys_hbm, near_queries_hbm,
+    tokens, masked, embed, w_qkv_hbm, w_out_hbm, cotangent_hbm, near_keys_hbm, near_queries_hbm,
     from_given, to_given, to_piece, to_middle_hbm,
     block_out, grad_tokens, gq, go, gm,
-    w_qkv, w_out, cotangent, near_keys, near_queries, to_middle, xm, g, key_bias, query_bias, hits, ctx, dqkv,
-    pieces, stacked, ext, g_pieces, g_stacked, g_ext,
-    stats, stat_pieces, stat_stacked, stat_ext, stat_rows, q, d, kv, own_kv, ext_q, ext_d,
-    total, made_a, made_b, got_a, got_b, *rest,
+    w_qkv, w_out, cotangent, key_bias, query_bias, to_middle, xm, g, hits, ctx, dqkv,
+    pieces, stacked, ext, g_stacked, g_ext,
+    stats, stat_pieces, stat_stacked, stat_ext, stat_rows, q, d, kv, own_kv, ext_q,
+    total, xm_t, made_a, made_b, got_a, got_b, *rest,
 ):
     scratch = [rest[5 * i : 5 * i + 5] for i in range(len(JOBS))]
     final_a, final_b, cross_a, cross_b, load, send, recv = rest[5 * len(JOBS) :]
@@ -129,8 +129,8 @@
 
     loaded = (
         (cotangent_hbm, cotangent),
-        (near_keys_hbm, near_keys),
-        (near_queries_hbm, near_queries),
+        (near_keys_hbm, key_bias),
+        (near_queries_hbm, query_bias),
         (to_middle_hbm, to_middle),
         (w_qkv_hbm, w_qkv),
         (w_out_hbm, w_out),
@@ -139,7 +139,9 @@
     for copy in loads:
         copy.start()
 
-    found = jnp.where(masked[0] == place[...], 1.0, 0.0)
+    place = lax.broadcasted_iota(jnp.int32, (288, 1), 0)
+    place = lax.rem(place, 2) * 144 + lax.div(lax.rem(place, 24), 2) * 12 + lax.div(place, 24)
+    found = jnp.where(masked[0] == place, 1.0, 0.0)
     hit = jnp.max(found, axis=-1, keepdims=True) > 0.5
     hits[...] = jnp.where(hit, 1.0, 0.0) + jnp.zeros((288, 128), F32)
     own_tokens = dot(from_given[...], tokens[...].reshape(288, 1024))
@@ -195,7 +197,7 @@
 
     rows_moved = to_neighbours(pieces, stacked, 0)
     sides_moved = to_sides(ext, 2)
-    g_rows_moved = to_neighbours(g_pieces, g_stacked, 4)
+    g_rows_moved = to_neighbours(pieces, g_stacked, 4)
     g_sides_moved = to_sides(g_ext, 6)
     stat_rows_moved = to_neighbours(stat_pieces, stat_stacked, 8)
     stat_sides_moved = to_sides(stat_ext, 10)
@@ -203,15 +205,15 @@
 
     finish(loads[:4])
     g[...] = dot(from_given[...], cotangent[...].reshape(288, 1024)).astype(BF16)
-    g_pieces[...] = dot(to_piece[...], g[...]).astype(BF16)
     g_stacked[144:432, :] = g[...]
     total[...] = g[...].astype(F32)
+    xm_t[...] = xm[...].T
     stats[...] = jnp.zeros((288, 128), F32)
     ext_row = lax.broadcasted_iota(jnp.int32, (1, 768), 1)
     ext_row = lax.div(lax.rem(ext_row, 48), 2) + lat * 12 - 6
     on_grid = (ext_row >= 0) & (ext_row < 96)
-    key_bias[...] = jnp.where(on_grid, near_keys[...], -jnp.inf)
-    query_bias[...] = jnp.where(on_grid, near_queries[...], -jnp.inf)
+    key_bias[...] = jnp.where(on_grid, key_bias[...], -jnp.inf)
+    query_bias[...] = jnp.where(on_grid, query_bias[...], -jnp.inf)
     finish(loads[4:])
 
     @pl.loop(0, 4)
@@ -225,27 +227,25 @@
     finish(rows_moved)
     ext[288:864, :] = dot(to_middle[...], stacked[...]).astype(BF16)
     begin(sides_moved)
-
-    def project(start, rows):
-        @pl.loop(0, 8)
+    pieces[...] = dot(to_piece[...], g[...]).astype(BF16)
+
+    def project(tiles, target, first_tile, middle):
+        @pl.loop(0, tiles)
         def _(t):
-            kv[start : start + rows, tile(t)] = dot(
-                ext[start : start + rows, :], w_qkv[:, tile(t, 1024)]
-            ).astype(BF16)
-
-    def project_queries(start, rows):
-        @pl.loop(0, 4)
-        def _(t):
-            ext_q[start : start + rows, tile(t)] = dot(
-                ext[start : start + rows, :], w_qkv[:, tile(t)]
-            ).astype(BF16)
-
-    project(288, 576)
-    project_queries(288, 576)
+            weights = w_qkv[:, tile(t, first_tile * 256)]
+            if middle:
+                target[288:864, tile(t)] = dot(ext[288:864, :], weights).astype(BF16)
+            else:
+                sides = jnp.concatenate([ext[0:288, :], ext[864:1152, :]], axis=0)
+                sides = dot(sides, weights).astype(BF16)
+                target[0:288, tile(t)] = sides[0:288]
+                target[864:1152, tile(t)] = sides[288:576]
+
+    project(8, kv, 4, True)
+    project(4, ext_q, 0, True)
     finish(sides_moved)
     begin(g_rows_moved)
-    project(0, 288)
-    project(864, 288)
+    project(8, kv, 4, False)
 
     lane_head = lax.div(lax.broadcasted_iota(jnp.int32, (96, 256), 1), 64)
     picks = [lane_head == h for h in range(4)]
@@ -265,10 +265,9 @@
     def queries(t):
         cols, vcols = tile(t), tile(t, 1024)
 
-        @pl.loop(0, 3)
-        def _(j):
-            rows = pl.ds(pl.multiple_of(j * 96, 96), 96)
-            keys = pl.ds(pl.multiple_of(j * 192, 192), 768)
+        for j in range(3):
+            rows = pl.ds(j * 96, 96)
+            keys = pl.ds(j * 192, 768)
             qm, dm = apart(q[rows, cols]), apart(d[rows, cols])
             kw, vw = kv[keys, cols], kv[keys, vcols]
             s = dot_nt(qm, kw).reshape(4, 96, 768) + key_bias[...][None]
@@ -291,12 +290,11 @@
     def keys_of(t):
         cols, vcols = tile(t), tile(t, 1024)
 
-        @pl.loop(0, 3)
-        def _(j):
-            rows = pl.ds(pl.multiple_of(j * 96, 96), 96)
-            seen = pl.ds(pl.multiple_of(j * 192, 192), 768)
+        for j in range(3):
+            rows = pl.ds(j * 96, 96)
+            seen = pl.ds(j * 192, 768)
             km, vm = apart(own_kv[rows, cols]), apart(own_kv[rows, vcols])
-            qw, dw = ext_q[seen, cols], ext_d[seen, cols]
+            qw, dw = ext_q[seen, cols], kv[seen, cols]
             known = stat_rows[j, 16 * t : 16 * t + 16, :]
             top, share, delta = (known[4 * i : 4 * i + 4].reshape(4, 1, 768) for i in range(3))
             s = dot_nt(km, qw).reshape(4, 96, 768) + query_bias[...][None]
@@ -333,29 +331,25 @@
     def columns(job):
         return pl.ds(JOBS[job][1], JOBS[job][2])
 
+    def store_made(made, half, cols, value):
+        made[half, :, :, :, :, :, cols] = value.astype(BF16).reshape(4, 2, 2, 4, 16, 256)
+
     def make_a(half):
-        def store(t, value):
-            made_a[half, t] = value.astype(BF16).reshape(2, 2, 4, 16, 1024)
-
         @pl.when(half == 0)
         def _():
             @pl.loop(0, 4)
             def _(t):
-                store(t, dot_tn(xm[:, tile(t)], dqkv[:, 0:1024]))
+                store_made(made_a, half, tile(t), dot(xm_t[...], dqkv[:, tile(t)]))
 
         @pl.when(half == 1)
         def _():
             @pl.loop(0, 4)
             def _(t):
-                store(t, dot_tn(ctx[:, tile(t)], g[...]))
+                store_made(made_a, half, tile(t), dot_tn(ctx[...], g[:, tile(t)]))
 
     def make_b(n, half):
         cols = pl.ds(pl.multiple_of(half * 1024 + 1024 + 256 * n, 256), 256)
-
-        @pl.loop(0, 4)
-        def _(t):
-            value = dot_tn(xm[:, tile(t)], dqkv[:, cols]).astype(BF16)
-            made_b[half, t, :, :, :, :, 256 * n : 256 * n + 256] = value.reshape(2, 2, 4, 16, 256)
+        store_made(made_b, half, pl.ds(256 * n, 256), dot(xm_t[...], dqkv[:, cols]))
 
     def exchange(job):
         where = (EVERY,) * 5 + (columns(job),)
@@ -426,8 +420,7 @@
     for job in (0, 1, 2):
         exchange(job).start()
 
-    project_queries(0, 288)
-    project_queries(864, 288)
+    project(4, ext_q, 0, False)
     finish(stat_rows_moved)
     stat_ext[288:864, :] = reordered(to_middle[...], stat_stacked[...])
     finish(g_sides_moved)
@@ -438,7 +431,7 @@
 
     @pl.loop(0, 4)
     def _(t):
-        ext_d[:, tile(t)] = dot_nt(g_ext[...], w_out[tile(t), :]).astype(BF16)
+        kv[:, tile(t)] = dot_nt(g_ext[...], w_out[tile(t), :]).astype(BF16)
 
     finish(stat_sides_moved)
     for j in range(3):
@@ -472,11 +465,10 @@
     add_to_total(2)
     exchanged(5)
     keys_of(3)
-    group(3)
-    advance((3, 1), (4, 0))
+    make_b(3, 1 - core)
+    for job in OF_QUAD[3]:
+        exchange(job).start()
     add_to_total(3)
-    exchanged(6)
-    exchanged(7)
 
     @pl.loop(0, 4)
     def _(t):
@@ -491,10 +483,12 @@
         made_b[1, t, :, :, :, :, 1024:1152] = column
 
     exchange(8).start()
-    advance((0, 2), (1, 2), (2, 2))
+    make_b(3, core)
+    exchanged(6)
+    exchanged(7)
+    exchanged(8)
+    advance((3, 1), (4, 0), (5, 0), (0, 2), (1, 2), (2, 2))
     swap(0).start()
-    advance((4, 1), (5, 0))
-    exchanged(8)
 
     @pl.loop(0, 4)
     def _(t):
@@ -505,8 +499,8 @@
         kept = dot(to_given[...], kept).astype(BF16)
         grad_tokens[:, :, :, cols] = kept.reshape(12, 12, 2, 256)
 
-    advance((3, 2), (6, 0), (7, 0), (5, 1), (8, 0), (4, 2), (6, 1), (7, 1), (8, 1))
-    advance((5, 2), (6, 2), (7, 2), (8, 2))
+    advance((6, 0), (7, 0), (8, 0), (4, 1), (5, 1), (3, 2), (6, 1), (7, 1), (8, 1))
+    advance((4, 2), (5, 2), (6, 2), (7, 2), (8, 2))
     swap(1).start()
     swap(0).wait()
     swap(1).wait()
@@ -540,9 +534,6 @@
     given = one_hot(given_order(), 288)
     piece, middle = one_hot(piece_order(), 288), one_hot(middle_order(), 576)
     orders = [given, given.T, piece, middle]
-    row, lev = np.arange(288) % 24 // 2, np.arange(288) % 2
-    place = lev * 144 + row * 12 + np.arange(288) // 24
-    place = np.broadcast_to(place[:, None], (288, 144)).astype(np.int32)
     vmem, hbm = pl.BlockSpec(memory_space=pltpu.VMEM), pl.BlockSpec(memory_space=pl.ANY)
     jobs = []
     for _, _, wide, order in JOBS:
@@ -560,7 +551,7 @@
             jax.ShapeDtypeStruct((8, 1024), F32),
             jax.ShapeDtypeStruct((8, 128), F32),
         ),
-        in_specs=[vmem] * 4 + [hbm] * 5 + [vmem] * 3 + [hbm],
+        in_specs=[vmem] * 3 + [hbm] * 5 + [vmem] * 3 + [hbm],
         out_specs=(vmem,) * 5,
         scratch_shapes=[
             pltpu.VMEM((1024, 3072), BF16),
@@ -571,15 +562,12 @@
             pltpu.VMEM((576, 576), BF16),
             pltpu.VMEM((288, 1024), BF16),
             pltpu.VMEM((288, 1024), BF16),
-            pltpu.VMEM((96, 768), F32),
-            pltpu.VMEM((96, 768), F32),
             pltpu.VMEM((288, 128), F32),
             pltpu.VMEM((288, 1024), BF16),
             pltpu.VMEM((288, 3072), BF16),
             pltpu.VMEM((288, 1024), BF16),
             pltpu.VMEM((576, 1024), BF16),
             pltpu.VMEM((1152, 1024), BF16),
-            pltpu.VMEM((288, 1024), BF16),
             pltpu.VMEM((576, 1024), BF16),
             pltpu.VMEM((1152, 1024), BF16),
             pltpu.VMEM((288, 128), F32),
@@ -592,8 +580,8 @@
             pltpu.VMEM((1152, 2048), BF16),
             pltpu.VMEM((288, 2048), BF16),
             pltpu.VMEM((1152, 1024), BF16),
-            pltpu.VMEM((1152, 1024), BF16),
             pltpu.VMEM((288, 1024), F32),
+            pltpu.VMEM((1024, 288), BF16),
             pltpu.VMEM((2, 4, 2, 2, 4, 16, 1024), BF16),
             pltpu.VMEM((2, 4, 2, 2, 4, 16, 1152), BF16),
             pltpu.VMEM((4, 2, 2, 4, 16, 1024), BF16),
@@ -608,11 +596,11 @@
             pltpu.SemaphoreType.DMA((14 + 10 * len(JOBS),)),
         ],
         compiler_params=pltpu.CompilerParams(
-            collective_id=1, has_side_effects=True, vmem_limit_bytes=62 * 1024 * 1024
+            collective_id=1, has_side_effects=True, vmem_limit_bytes=63 * 1024 * 1024
         ),
         name="attention_block",
     )(
-        tokens.transpose(1, 2, 0, 3), masked, jnp.asarray(place), mask_embed.reshape(8, 128), w_qkv, w_out,
+        tokens.transpose(1, 2, 0, 3), masked, mask_embed.reshape(8, 128), w_qkv, w_out,
         cotangent.transpose(1, 2, 0, 3), jnp.asarray(near(0)), jnp.asarray(near(1)),
         *[jnp.asarray(order, BF16) for order in orders],
     )

time: 127 us -> 116 us (0.913)
  Pallas kernels: 126 us -> 115 us
    pallas_call x1, Pallas kernels: 124 us -> 113 us  [local(): pl.pallas_call(block_kernel, out_shape=(jax.ShapeDtypeStruct((12, 12, 2,...]
where the time goes in v4:
time: 116 us
  Pallas kernels  115 us (99%)
    pallas_call x1, Pallas kernels, local(): pl.pallas_call(block_kernel, out_shape=(jax.ShapeDtypeStruct((12, 12, 2,...  113 us
    pallas_call x1, Pallas kernels, local(): pl.pallas_call(hand_out_kernel, out_shape=(jax.ShapeDtypeStruct((12, 12,...  2.35 us

profile of v4, /device:TPU:1, one launch (start us, length us, event | category | flops | bytes accessed | tf_op | source)
XLA Modules:
  0.0 116.0 jit_solution(12873448481372391268)
XLA Ops:
  0.6 113.0 %attention_block.1 = (bf16[12,12,2,1024]{3,2,1,0:T(2,128)(2,1)}, bf16[12,12,2,1024]{3,2,1,0:T(2,128)(2,1)}, f32[8,3072]{1,0:T(8,128)}, f32[8,1024]{1,0:T(8,128)}, f32[8,128]{1,0:T(8,128)}) custom-call(bf16[12,12,2,1024]{3,2,1,0:T(2,128)(2,1)} %bitcast.5, s32[1,1,144]{2,1,0:T(1,128)} %masked.1, bf16[8,128]{1,0:T(8,128)(2,1)} %bitcast.7, ...), custom_call_target="tpu_custom_call" | custom-call | tf_op jit(solution)/shard_map/attention_block/pallas_call | solution.py:545
  113.6 2.3 %hand_out.1 = (bf16[12,12,2,1024]{3,2,1,0:T(2,128)(2,1)}, bf16[12,12,2,1024]{3,2,1,0:T(2,128)(2,1)}, f32[8,3072]{1,0:T(8,128)}, f32[8,1024]{1,0:T(8,128)}, f32[8]{0:T(128)}) custom-call(bf16[12,12,2,1024]{3,2,1,0:T(2,128)(2,1)} %get-tuple-element.15.block_out, bf16[12,12,2,1024]{3,2,1,0:T(2,128)(2,1)} %get-tuple-element.16.grad_tokens, ...), custom_call_target="tpu_custom_call" | custom-call | tf_op jit(solution)/shard_map/hand_out/pallas_call | solution.py:607

commit v5 on v4

--- a/solution.py
+++ b/solution.py
@@ -23,8 +23,8 @@
     (1, 256, 256, "zyx"),
     (1, 512, 256, "yxz"),
     (1, 768, 128, "xzy"),
-    (1, 896, 128, "yxz"),
-    (1, 1024, 128, "zyx"),
+    (1, 896, 128, "zyx"),
+    (1, 1024, 128, "yxz"),
 )
 OF_QUAD = ((3,), (4,), (5,), (6, 7))
 
@@ -93,11 +93,11 @@
 def block_kernel(
     tokens, masked, embed, w_qkv_hbm, w_out_hbm, cotangent_hbm, near_keys_hbm, near_queries_hbm,
     from_given, to_given, to_piece, to_middle_hbm,
-    block_out, grad_tokens, gq, go, gm,
-    w_qkv, w_out, cotangent, key_bias, query_bias, to_middle, xm, g, hits, ctx, dqkv,
+    block_out_hbm, grad_tokens_hbm, gq, go, gm,
+    block_out, grad_tokens, w_qkv, w_out, cotangent, key_bias, query_bias, to_middle, xm, g, hits, ctx, dqkv,
     pieces, stacked, ext, g_stacked, g_ext,
     stats, stat_pieces, stat_stacked, stat_ext, stat_rows, q, d, kv, own_kv, ext_q,
-    total, xm_t, made_a, made_b, got_a, got_b, *rest,
+    total, xm_t, ctx_t, made_a, made_b, got_a, got_b, *rest,
 ):
     scratch = [rest[5 * i : 5 * i + 5] for i in range(len(JOBS))]
     final_a, final_b, cross_a, cross_b, load, send, recv = rest[5 * len(JOBS) :]
@@ -345,7 +345,7 @@
         def _():
             @pl.loop(0, 4)
             def _(t):
-                store_made(made_a, half, tile(t), dot_tn(ctx[...], g[:, tile(t)]))
+                store_made(made_a, half, tile(t), dot(ctx_t[...], g[:, tile(t)]))
 
     def make_b(n, half):
         cols = pl.ds(pl.multiple_of(half * 1024 + 1024 + 256 * n, 256), 256)
@@ -416,6 +416,11 @@
             exchange(job).start()
         make_b(n, core)
 
+    ctx_t[...] = ctx[...].T
+    leaving = (
+        pltpu.make_async_copy(block_out, block_out_hbm, load.at[6]),
+        pltpu.make_async_copy(grad_tokens, grad_tokens_hbm, load.at[7]),
+    )
     make_a(1 - core)
     for job in (0, 1, 2):
         exchange(job).start()
@@ -457,9 +462,6 @@
     @pl.loop(0, 4)
     def _(t):
         cols = tile(t)
-        value = xm[:, cols].astype(F32) + dot(ctx[...], w_out[:, cols])
-        value = dot(to_given[...], value.astype(BF16)).astype(BF16)
-        block_out[:, :, :, cols] = value.reshape(12, 12, 2, 256)
         total[:, cols] += dot_nt(dqkv[:, 0:1024], w_qkv[cols, 0:1024])
 
     add_to_total(2)
@@ -499,9 +501,21 @@
         kept = dot(to_given[...], kept).astype(BF16)
         grad_tokens[:, :, :, cols] = kept.reshape(12, 12, 2, 256)
 
-    advance((6, 0), (7, 0), (8, 0), (4, 1), (5, 1), (3, 2), (6, 1), (7, 1), (8, 1))
+    leaving[1].start()
+    advance((6, 0), (7, 0), (8, 0))
+
+    @pl.loop(0, 4)
+    def _(t):
+        cols = tile(t)
+        value = xm[:, cols].astype(F32) + dot(ctx[...], w_out[:, cols])
+        value = dot(to_given[...], value.astype(BF16)).astype(BF16)
+        block_out[:, :, :, cols] = value.reshape(12, 12, 2, 256)
+
+    leaving[0].start()
+    advance((4, 1), (5, 1), (3, 2), (6, 1), (7, 1), (8, 1))
     advance((4, 2), (5, 2), (6, 2), (7, 2), (8, 2))
     swap(1).start()
+    finish(leaving)
     swap(0).wait()
     swap(1).wait()
     rows = pl.ds(pl.multiple_of(core * 8, 8), 8)
@@ -552,8 +566,10 @@
             jax.ShapeDtypeStruct((8, 128), F32),
         ),
         in_specs=[vmem] * 3 + [hbm] * 5 + [vmem] * 3 + [hbm],
-        out_specs=(vmem,) * 5,
+        out_specs=(hbm, hbm, vmem, vmem, vmem),
         scratch_shapes=[
+            pltpu.VMEM((12, 12, 2, 1024), BF16),
+            pltpu.VMEM((12, 12, 2, 1024), BF16),
             pltpu.VMEM((1024, 3072), BF16),
             pltpu.VMEM((1024, 1024), BF16),
             pltpu.VMEM((12, 12, 2, 1024), BF16),
@@ -582,6 +598,7 @@
             pltpu.VMEM((1152, 1024), BF16),
             pltpu.VMEM((288, 1024), F32),
             pltpu.VMEM((1024, 288), BF16),
+            pltpu.VMEM((1024, 288), BF16),
             pltpu.VMEM((2, 4, 2, 2, 4, 16, 1024), BF16),
             pltpu.VMEM((2, 4, 2, 2, 4, 16, 1152), BF16),
             pltpu.VMEM((4, 2, 2, 4, 16, 1024), BF16),
@@ -591,7 +608,7 @@
             pltpu.VMEM((16, 1152), F32),
             pltpu.VMEM((8, 1024), F32),
             pltpu.VMEM((8, 1024), F32),
-            pltpu.SemaphoreType.DMA((6,)),
+            pltpu.SemaphoreType.DMA((8,)),
             pltpu.SemaphoreType.DMA((14 + 10 * len(JOBS),)),
             pltpu.SemaphoreType.DMA((14 + 10 * len(JOBS),)),
         ],

time: 116 us -> 113 us (0.974)
  Pallas kernels: 115 us -> 112 us
    pallas_call x1, Pallas kernels: 113 us -> 110 us  [local(): pl.pallas_call(block_kernel, out_shape=(jax.ShapeDtypeStruct((12, 12, 2,...]
where the time goes in v5:
time: 113 us
  Pallas kernels  112 us (99%)
    pallas_call x1, Pallas kernels, local(): pl.pallas_call(block_kernel, out_shape=(jax.ShapeDtypeStruct((12, 12, 2,...  110 us
    pallas_call x1, Pallas kernels, local(): pl.pallas_call(hand_out_kernel, out_shape=(jax.ShapeDtypeStruct((12, 12,...  2.35 us

profile of v5, /device:TPU:1, one launch (start us, length us, event | category | flops | bytes accessed | tf_op | source)
XLA Modules:
  0.0 112.7 jit_solution(4666299118584445379)
XLA Ops:
  0.6 109.7 %attention_block.1 = (bf16[12,12,2,1024]{3,2,1,0:T(2,128)(2,1)}, bf16[12,12,2,1024]{3,2,1,0:T(2,128)(2,1)}, f32[8,3072]{1,0:T(8,128)}, f32[8,1024]{1,0:T(8,128)}, f32[8,128]{1,0:T(8,128)}) custom-call(bf16[12,12,2,1024]{3,2,1,0:T(2,128)(2,1)} %bitcast.5, s32[1,1,144]{2,1,0:T(1,128)} %masked.1, bf16[8,128]{1,0:T(8,128)(2,1)} %bitcast.7, ...), custom_call_target="tpu_custom_call" | custom-call | tf_op jit(solution)/shard_map/attention_block/pallas_call | solution.py:559
  110.4 2.3 %hand_out.1 = (bf16[12,12,2,1024]{3,2,1,0:T(2,128)(2,1)}, bf16[12,12,2,1024]{3,2,1,0:T(2,128)(2,1)}, f32[8,3072]{1,0:T(8,128)}, f32[8,1024]{1,0:T(8,128)}, f32[8]{0:T(128)}) custom-call(bf16[12,12,2,1024]{3,2,1,0:T(2,128)(2,1)} %get-tuple-element.15.block_out, bf16[12,12,2,1024]{3,2,1,0:T(2,128)(2,1)} %get-tuple-element.16.grad_tokens, ...), custom_call_target="tpu_custom_call" | custom-call | tf_op jit(solution)/shard_map/hand_out/pallas_call | solution.py:624

commit v6 on v5

--- a/solution.py
+++ b/solution.py
@@ -145,7 +145,8 @@
     hit = jnp.max(found, axis=-1, keepdims=True) > 0.5
     hits[...] = jnp.where(hit, 1.0, 0.0) + jnp.zeros((288, 128), F32)
     own_tokens = dot(from_given[...], tokens[...].reshape(288, 1024))
-    mask_row = jnp.concatenate([embed[i : i + 1, :] for i in range(8)], axis=1).astype(F32)
+    mask_rows = embed[...].astype(F32)
+    mask_row = jnp.concatenate([mask_rows[i : i + 1] for i in range(8)], axis=1)
     xm[...] = jnp.where(hit, mask_row, own_tokens).astype(BF16)
 
     pieces[...] = dot(to_piece[...], xm[...]).astype(BF16)

time: 113 us -> 113 us (level)
  no operation moved by 1% of the time
where the time goes in v6:
time: 113 us
  Pallas kernels  112 us (99%)
    pallas_call x1, Pallas kernels, local(): pl.pallas_call(block_kernel, out_shape=(jax.ShapeDtypeStruct((12, 12, 2,...  110 us
    pallas_call x1, Pallas kernels, local(): pl.pallas_call(hand_out_kernel, out_shape=(jax.ShapeDtypeStruct((12, 12,...  2.35 us

profile of v6, /device:TPU:1, one launch (start us, length us, event | category | flops | bytes accessed | tf_op | source)
XLA Modules:
  0.0 112.7 jit_solution(17955090773093572759)
XLA Ops:
  0.6 109.7 %attention_block.1 = (bf16[12,12,2,1024]{3,2,1,0:T(2,128)(2,1)}, bf16[12,12,2,1024]{3,2,1,0:T(2,128)(2,1)}, f32[8,3072]{1,0:T(8,128)}, f32[8,1024]{1,0:T(8,128)}, f32[8,128]{1,0:T(8,128)}) custom-call(bf16[12,12,2,1024]{3,2,1,0:T(2,128)(2,1)} %bitcast.5, s32[1,1,144]{2,1,0:T(1,128)} %masked.1, bf16[8,128]{1,0:T(8,128)(2,1)} %bitcast.7, ...), custom_call_target="tpu_custom_call" | custom-call | tf_op jit(solution)/shard_map/attention_block/pallas_call | solution.py:560
  110.4 2.3 %hand_out.1 = (bf16[12,12,2,1024]{3,2,1,0:T(2,128)(2,1)}, bf16[12,12,2,1024]{3,2,1,0:T(2,128)(2,1)}, f32[8,3072]{1,0:T(8,128)}, f32[8,1024]{1,0:T(8,128)}, f32[8]{0:T(128)}) custom-call(bf16[12,12,2,1024]{3,2,1,0:T(2,128)(2,1)} %get-tuple-element.15.block_out, bf16[12,12,2,1024]{3,2,1,0:T(2,128)(2,1)} %get-tuple-element.16.grad_tokens, ...), custom_call_target="tpu_custom_call" | custom-call | tf_op jit(solution)/shard_map/hand_out/pallas_call | solution.py:625
